TPU v7x, 32 devices: a whole 2x2x4 slice. The times are simulated.
32 devices in a mesh: fsdp: 16 (over z, x, core), expert: 2 (over y).
Axes of the slice: x: 2, y: 2, z: 4, core: 2. Of those that a mesh axis runs over, the one named last changes fastest.
Arguments:
- prompt_in: bfloat16 [16, 1024, 768], P('fsdp', 'expert'), may hold values from -6 to 6
- cont_in: bfloat16 [16, 2, 512, 768], P('fsdp', 'expert'), may hold values from -6 to 6
- prompt_cot: bfloat16 [16, 1024, 768], P('fsdp', 'expert'), may hold values from -6 to 6
- cont_cot: bfloat16 [16, 2, 512, 768], P('fsdp', 'expert'), may hold values from -6 to 6
- prompt_route: int32 [16, 1024, 2], P('fsdp', 'expert'), may hold values from 0 to 7, all different within a row
- cont_route: int32 [16, 2, 512, 2], P('fsdp', 'expert'), may hold values from 0 to 7, all different within a row
- rel_bucket: int32 [1536], replicated, may hold values from 0 to 31
- norm_attn: bfloat16 [768], P('fsdp'), may hold values from 0.25 to 1.75
- norm_ffn: bfloat16 [768], P('fsdp'), may hold values from 0.25 to 1.75
- w_qkv: bfloat16 [768, 2304], P('fsdp'), may hold values from -0.21875 to 0.21875
- w_out: bfloat16 [768, 768], P('fsdp'), may hold values from -0.875 to 0.875
- rel_w: bfloat16 [32, 12], P('fsdp'), may hold values from -4 to 4
- w_router: bfloat16 [768, 8], P('fsdp'), may hold values from -0.14941406 to 0.14941406
- expert_in: bfloat16 [8, 768, 3072], P('expert', 'fsdp'), may hold values from -0.21875 to 0.21875
- expert_out: bfloat16 [8, 3072, 768], P('expert', 'fsdp'), may hold values from -0.15625 to 0.15625
Outputs:
- prompt_out: bfloat16 [16, 1024, 768], P('fsdp', 'expert')
- cont_out: bfloat16 [16, 2, 512, 768], P('fsdp', 'expert')
- prompt_grad: float32 [16, 1024, 768], P('fsdp', 'expert')
- cont_grad: float32 [16, 2, 512, 768], P('fsdp', 'expert')
- grad_norm_attn: float32 [768], P('fsdp')
- grad_norm_ffn: float32 [768], P('fsdp')
- grad_qkv: float32 [768, 2304], P('fsdp')
- grad_out: float32 [768, 768], P('fsdp')
- grad_rel: float32 [32, 12], P('fsdp')
- grad_router: float32 [768, 8], P('fsdp')
- grad_expert_in: float32 [8, 768, 3072], P('expert', 'fsdp')
- grad_expert_out: float32 [8, 3072, 768], P('expert', 'fsdp')
Inputs may be any that keep to these rules, and one draw needn't show every extreme that they name: `prompt_route`: each row names two different experts. `cont_route`: each row names two different experts.
All inputs are finite; a program needn't handle non-finite values.
Results may differ from a plain program's by a relative error of at most 0.03.
Values may be sent and summed in bfloat16 or wider, within the bound.
A program may use at most 512 MiB of HBM per device.

v0:
```python
import functools

import jax
import jax.numpy as jnp
from jax import lax
from jax.experimental import pallas as pl
from jax.experimental.pallas import tpu as pltpu
from jax.sharding import PartitionSpec as P

epsilon = 1e-06
blocked = -1e30
f32 = jnp.float32
bf16 = jnp.bfloat16
KB = 128
VMEM_LIMIT = 60 * 1024 * 1024


def nn(a, b):
    return lax.dot_general(a, b, (((1,), (0,)), ((), ())), preferred_element_type=f32)


def nt(a, b):
    return lax.dot_general(a, b, (((1,), (1,)), ((), ())), preferred_element_type=f32)


def tn(a, b):
    return lax.dot_general(a, b, (((0,), (0,)), ((), ())), preferred_element_type=f32)


def make_strips(table_ref, strip_ref):
    width = strip_ref.shape[2]
    for h in range(2):
        wide = jnp.broadcast_to(table_ref[0, h : h + 1, :], (KB, width))
        strip_ref[h] = pltpu.roll(wide, 0, 1, stride=1, stride_axis=0)


def query_sets(own, n_prompt, n_cont, group, most):
    prompt_len = group * n_prompt
    rows = n_prompt + n_cont
    place = [lax.rem(own + s, group) * n_prompt for s in range(group)]
    start = [0] + [rows + s * n_prompt for s in range(group - 1)]
    sets = []
    for base, count, first_place in ((0, n_prompt, place[0]), (n_prompt, n_cont, prompt_len)):
        size = most if count % most == 0 else count
        for first in range(0, count, size):
            keys = [(base, first + size, prompt_len + first)]
            for s in range(group):
                if base or s:
                    keys.append((start[s], n_prompt, prompt_len + first_place + first - place[s]))
            sets.append((base + first, size, keys))
    return sets


def strip_window(strip_ref, h, offset, keys, rows):
    parts = []
    for kb in range(keys // KB):
        start = offset - kb * KB
        if not isinstance(start, int):
            start = pl.multiple_of(start, KB)
        parts.append(strip_ref[h, :, pl.ds(start, rows)])
    return parts[0] if len(parts) == 1 else jnp.concatenate(parts, axis=0)


def head_lanes(x, h, head_size):
    lanes = lax.broadcasted_iota(jnp.int32, x.shape, 1)
    return jnp.where((lanes >= h * head_size) & (lanes < (h + 1) * head_size), x, jnp.zeros_like(x))


def attend_kernel(n_prompt, n_cont, group, head_size, own_ref, table_ref, q_ref, k_ref, v_ref, o_ref, lse_ref, strip_ref):
    make_strips(table_ref, strip_ref)
    scale = jnp.asarray(head_size**-0.5, bf16)
    for first, rows, keys in query_sets(own_ref[0], n_prompt, n_cont, group, 512):
        q_pair = q_ref[first : first + rows, :] * scale
        heads = []
        for h in range(2):
            q = head_lanes(q_pair, h, head_size)
            m = l = acc = None
            for start, count, offset in keys:
                s = nt(k_ref[start : start + count, :], q) + strip_window(strip_ref, h, offset, count, rows)
                top = jnp.max(s, axis=0, keepdims=True)
                m_new = top if m is None else jnp.maximum(m, top)
                p = jnp.exp(s - m_new)
                total = jnp.sum(p, axis=0, keepdims=True)
                out = tn(v_ref[start : start + count, :], p.astype(bf16))[h * head_size : (h + 1) * head_size]
                if m is None:
                    l, acc = total, out
                else:
                    shrink = jnp.exp(m - m_new)
                    l, acc = l * shrink + total, acc * shrink + out
                m = m_new
            heads.append(acc / l)
            lse_ref[0, h : h + 1, first : first + rows] = m + jnp.log(l)
        o_ref[first : first + rows, :] = jnp.concatenate(heads, axis=0).T.astype(bf16)


def attend_grad_kernel(n_prompt, n_cont, group, head_size, own_ref, table_ref, q_ref, k_ref, v_ref, o_ref, do_ref, lse_ref,
                       dqkv_ref, drel_ref, strip_ref, diag_ref, dk_ref, dv_ref):
    make_strips(table_ref, strip_ref)
    width = strip_ref.shape[2]
    mine = n_prompt + n_cont
    scale = jnp.asarray(head_size**-0.5, bf16)
    diag_ref[...] = jnp.zeros_like(diag_ref)
    dk_ref[...] = jnp.zeros_like(dk_ref)
    dv_ref[...] = jnp.zeros_like(dv_ref)
    for first, rows, keys in query_sets(own_ref[0], n_prompt, n_cont, group, 256):
        q_pair = q_ref[first : first + rows, :] * scale
        do_pair = do_ref[first : first + rows, :]
        inner = (do_pair.astype(f32) * o_ref[first : first + rows, :].astype(f32)).T
        heads = []
        for h in range(2):
            q = head_lanes(q_pair, h, head_size)
            do = head_lanes(do_pair, h, head_size)
            delta = jnp.sum(inner[h * head_size : (h + 1) * head_size], axis=0, keepdims=True)
            lse = lse_ref[0, h : h + 1, first : first + rows]
            dq = None
            for start, count, offset in keys:
                at = slice(start, start + count)
                k = k_ref[at, :]
                s = nt(k, q) + strip_window(strip_ref, h, offset, count, rows)
                p = jnp.exp(s - lse)
                ds = p * (nt(v_ref[at, :], do) - delta)
                for kb in range(count // KB):
                    lane = offset - kb * KB
                    if not isinstance(lane, int):
                        lane = pl.multiple_of(lane, KB)
                    diag_ref[h, :, pl.ds(lane, rows)] += ds[kb * KB : (kb + 1) * KB]
                ds = ds.astype(bf16)
                dv_ref[at, :] += nn(p.astype(bf16), do)
                dk_ref[at, :] += nn(ds, q)
                part = tn(k, ds)[h * head_size : (h + 1) * head_size]
                dq = part if dq is None else dq + part
            heads.append(dq)
        dqkv_ref[0, first : first + rows, :] = (jnp.concatenate(heads, axis=0).T * (head_size**-0.5)).astype(bf16)
    if dqkv_ref.shape[1] > mine:
        dqkv_ref[0, mine:, :] = jnp.zeros((dqkv_ref.shape[1] - mine, dqkv_ref.shape[2]), bf16)
    dqkv_ref[1] = dk_ref[...].astype(bf16)
    dqkv_ref[2] = dv_ref[...].astype(bf16)
    for h in range(2):
        x = diag_ref[h]
        half = KB // 2
        while half >= 8:
            x = x[:half] + pltpu.roll(x[half:], width - half, 1)
            half //= 2
        row = x[0:1]
        for i in range(1, 8):
            row = row + pltpu.roll(x[i : i + 1], width - i, 1)
        drel_ref[0, h : h + 1, :] = row


def attention_specs(rows, width, pairs):
    return [
        pl.BlockSpec((1, 2, width), lambda j, own: (j, 0, 0)),
        pl.BlockSpec((rows, 128), lambda j, own: (0, j)),
        pl.BlockSpec((rows, 128), lambda j, own: (0, pairs + j)),
        pl.BlockSpec((rows, 128), lambda j, own: (0, 2 * pairs + j)),
    ]


def attend(own, table, qkv, n_prompt, n_cont, group, head_size):
    pairs, _, width = table.shape
    mine = n_prompt + n_cont
    work = pairs * 2 * (n_prompt * n_prompt * group + n_cont * (n_prompt * group + n_cont))
    return pl.pallas_call(
        functools.partial(attend_kernel, n_prompt, n_cont, group, head_size),
        out_shape=(
            jax.ShapeDtypeStruct((mine, pairs * 128), bf16),
            jax.ShapeDtypeStruct((pairs, 2, mine), f32),
        ),
        grid_spec=pltpu.PrefetchScalarGridSpec(
            num_scalar_prefetch=1,
            grid=(pairs,),
            in_specs=attention_specs(qkv.shape[0], width, pairs),
            out_specs=(
                pl.BlockSpec((mine, 128), lambda j, own: (0, j)),
                pl.BlockSpec((1, 2, mine), lambda j, own: (j, 0, 0)),
            ),
            scratch_shapes=[pltpu.VMEM((2, KB, width), f32)],
        ),
        compiler_params=pltpu.CompilerParams(vmem_limit_bytes=VMEM_LIMIT),
        cost_estimate=pl.CostEstimate(flops=16 * work * head_size, bytes_accessed=16 * mine * pairs * 128, transcendentals=work),
        name="attend",
    )(own, table, qkv, qkv, qkv)


def attend_grad(own, table, qkv, heads_out, dheads, lse, n_prompt, n_cont, group, head_size):
    pairs, _, width = table.shape
    rows, mine = qkv.shape[0], n_prompt + n_cont
    work = pairs * 2 * (n_prompt * n_prompt * group + n_cont * (n_prompt * group + n_cont))
    return pl.pallas_call(
        functools.partial(attend_grad_kernel, n_prompt, n_cont, group, head_size),
        out_shape=(
            jax.ShapeDtypeStruct((3, rows, pairs * 128), bf16),
            jax.ShapeDtypeStruct((pairs, 2, width), f32),
        ),
        grid_spec=pltpu.PrefetchScalarGridSpec(
            num_scalar_prefetch=1,
            grid=(pairs,),
            in_specs=attention_specs(rows, width, pairs)
            + [
                pl.BlockSpec((mine, 128), lambda j, own: (0, j)),
                pl.BlockSpec((mine, 128), lambda j, own: (0, j)),
                pl.BlockSpec((1, 2, mine), lambda j, own: (j, 0, 0)),
            ],
            out_specs=(
                pl.BlockSpec((3, rows, 128), lambda j, own: (0, 0, j)),
                pl.BlockSpec((1, 2, width), lambda j, own: (j, 0, 0)),
            ),
            scratch_shapes=[
                pltpu.VMEM((2, KB, width), f32),
                pltpu.VMEM((2, KB, width), f32),
                pltpu.VMEM((rows, 128), f32),
                pltpu.VMEM((rows, 128), f32),
            ],
        ),
        compiler_params=pltpu.CompilerParams(vmem_limit_bytes=VMEM_LIMIT),
        cost_estimate=pl.CostEstimate(flops=40 * work * head_size, bytes_accessed=40 * mine * pairs * 128, transcendentals=work),
        name="attend_grad",
    )(own, table, qkv, qkv, qkv, heads_out, dheads, lse)


def unit_list(n_prompt, n_cont, cap_prompt, cap_cont, padded):
    if cap_prompt % 16 == 0 and cap_cont % 16 == 0:
        return ((0, n_prompt, 0, cap_prompt), (n_prompt, n_cont, cap_prompt, cap_cont))
    return ((0, n_prompt + n_cont, 0, padded),)


def slots_of(units, routes_ref, experts, padded, caps):
    found = []
    for (first, rows, slot), cap in zip(units, caps):
        numbers = lax.broadcasted_iota(jnp.int32, (experts, rows), 0)
        routes = [routes_ref[c : c + 1, first : first + rows] for c in range(2)]
        hits = [numbers == r for r in routes]
        both = jnp.where(hits[0] | hits[1], 1.0, 0.0).astype(bf16)
        before = lax.broadcasted_iota(jnp.int32, (rows, rows), 0) < lax.broadcasted_iota(jnp.int32, (rows, rows), 1)
        earlier = nn(both, jnp.where(before, 1.0, 0.0).astype(bf16))
        for c in range(2):
            count = jnp.sum(jnp.where(hits[c], earlier, 0.0), axis=0, keepdims=True).astype(jnp.int32)
            found.append(jnp.where(count < cap, routes[c] * padded + slot + count, -1))
    return found


def chosen_rows(target_ref, unit, experts, padded):
    first, rows, slot, slots = unit
    parts = []
    for e in range(experts):
        numbers = lax.broadcasted_iota(jnp.int32, (slots, rows), 0) + (e * padded + slot)
        hit = [numbers == target_ref[c : c + 1, first : first + rows] for c in range(2)]
        parts.append(jnp.where(hit[0] | hit[1], 1.0, 0.0).astype(bf16))
    return jnp.concatenate(parts, axis=0)


def target_columns(target_ref, unit):
    first, rows = unit[:2]
    turned = target_ref[:, first : first + rows].astype(f32).T.astype(jnp.int32)
    return [turned[:, c : c + 1] for c in range(2)]


def cots_kernel(units, caps, experts, padded, routes_ref, cot_refs, target_ref, out_ref):
    first_slot = 0
    row_units = []
    first = 0
    for rows, cap in caps:
        row_units.append((first, rows, first_slot))
        first, first_slot = first + rows, first_slot + cap
    found = slots_of(row_units, routes_ref, experts, padded, [cap for _, cap in caps])
    target_ref[...] = jnp.full(target_ref.shape, -1, jnp.int32)
    for u, (first, rows, _) in enumerate(row_units):
        for c in range(2):
            target_ref[c : c + 1, first : first + rows] = found[2 * u + c]
    for unit in units:
        first, rows, slot, slots = unit
        cot = jnp.concatenate([ref[...] for ref in cot_refs], axis=0) if len(units) == 1 else cot_refs[1 if first else 0][...]
        got = nn(chosen_rows(target_ref, unit, experts, padded), cot).astype(bf16)
        for e in range(experts):
            out_ref[e, slot : slot + slots, :] = got[e * slots : (e + 1) * slots]


def remote(src, dst, device, send_sem, recv_sem):
    return pltpu.make_async_remote_copy(
        src_ref=src, dst_ref=dst, send_sem=send_sem, recv_sem=recv_sem, device_id=device, device_id_type=pl.DeviceIdType.MESH
    )


def greet(devices):
    barrier = pltpu.get_barrier_semaphore()
    for device in devices:
        pl.semaphore_signal(barrier, inc=1, device_id=device, device_id_type=pl.DeviceIdType.MESH)
    pl.semaphore_wait(barrier, len(devices))


def look_up(table, i):
    found = jnp.int32(table[0])
    for j in range(1, len(table)):
        found = jnp.where(i == j, jnp.int32(table[j]), found)
    return found


def ring_places(cycle):
    count = len(cycle)
    inverse = [0] * count
    for p, c in enumerate(cycle):
        inverse[c] = p
    team = lax.axis_index("team")
    place = look_up(inverse, lax.axis_index("depth") * 2 + team // 2)

    def chip(distance):
        return look_up(cycle, lax.rem(place + (distance + count), count))

    def device(chip, core):
        return {"depth": chip // 2, "team": lax.rem(chip, 2) * 2 + core}

    return chip, device, lax.rem(team, 2)


def ring_pieces(cut, qkv, wout, extra):
    return ((qkv, slice(0, cut), 0), (qkv, slice(cut, qkv.shape[-1]), 1), (wout, slice(0, wout.shape[-1]), 1), (extra, slice(0, extra.shape[-1]), 1))


def ring_gather(cycle, cut, hops_from, hops_to, shards, outs, sems, between=()):
    ring_send, ring_recv, core_send, core_recv = sems
    count = len(cycle)
    chip, at, core = ring_places(cycle)
    right, left, partner = at(chip(1), core), at(chip(-1), core), {"team": lax.axis_index("team") + 1 - 2 * core}
    pieces = ring_pieces(cut, *outs)
    long, short = count // 2, count - 1 - count // 2
    streams = ((0, right, -1, long), (1, left, 1, long), (0, left, 1, short), (1, right, -1, short))
    started, arrivals = [], []

    def start(copy):
        copy.start()
        started.append(copy)

    def slot(p, c, k):
        return pieces[p][0].at[c, k, :, pieces[p][1]]

    def source(p, c):
        return slot(p, c, core) if shards is None else ring_pieces(cut, *shards)[p][0].at[:, pieces[p][1]]

    def hop_copies(k, c, hop, first=False):
        half, device = streams[k][:2]
        return [
            remote(source(p, c) if first else slot(p, c, core), slot(p, c, core), device, ring_send.at[k, hop, p], ring_recv.at[k, hop, p])
            for p in range(len(pieces))
            if pieces[p][2] == half
        ]

    def across(c, half, first=False):
        for p in range(len(pieces)):
            if pieces[p][2] == half:
                number = len(arrivals)
                start(remote(source(p, c) if first else slot(p, c, core), slot(p, c, core), partner, core_send.at[number], core_recv.at[number]))
                arrivals.append(slot(p, c, 1 - core))

    for k, (half, device, sign, hops) in enumerate(streams):
        if hops_from < hops:
            for copy in hop_copies(k, chip(sign * hops_from), hops_from, hops_from == 0):
                start(copy)
    if hops_from == 0:
        for half in range(2):
            across(chip(0), half, True)
    for action in between:
        action()
    for hop in range(hops_from, hops_to):
        for k, (half, device, sign, hops) in enumerate(streams):
            if hop < hops:
                other = chip(sign * (1 + hop))
                for copy in hop_copies(k, other, hop):
                    copy.wait_recv()
                if hop + 1 < min(hops, hops_to):
                    for copy in hop_copies(k, other, hop + 1):
                        start(copy)
                across(other, half)
    waits = [remote(v, v, partner, core_send.at[n], core_recv.at[n]).wait_recv for n, v in enumerate(arrivals)]
    return waits + [copy.wait_send for copy in started]


def ring_neighbours(cycle):
    chip, at, core = ring_places(cycle)
    return [at(chip(1), core), at(chip(-1), core), {"team": lax.axis_index("team") + 1 - 2 * core}]


def front_kernel(cycle, cut, hops, qkv_ref, wout_ref, extra_ref, win_ref, qkv_out, wout_out, extra_out, win_out,
                 ring_send, ring_recv, core_send, core_recv, team_send, team_recv, local_sem):
    chip, _, core = ring_places(cycle)
    team = lax.axis_index("team")
    mates = [team + d - 4 * ((team + d) // 4) for d in range(1, 4)]
    greet(ring_neighbours(cycle) + [{"team": t} for t in mates])
    waits = []

    def swap():
        for d, t in enumerate(mates):
            copy = remote(win_ref.at[t], win_out.at[team], {"team": t}, team_send.at[d], team_recv.at[d])
            copy.start()
            source = team + 3 - d - 4 * ((team + 3 - d) // 4)
            waits.append(remote(win_ref.at[t], win_out.at[source], {"team": t}, team_send.at[d], team_recv.at[d]).wait_recv)
            waits.append(copy.wait_send)
        keep = [(win_ref.at[team], win_out.at[team])]
        keep += [(src, out.at[chip(0), core]) for src, out in ((qkv_ref, qkv_out), (wout_ref, wout_out), (extra_ref, extra_out))]
        for p, (src, dst) in enumerate(keep):
            copy = pltpu.make_async_copy(src, dst, local_sem.at[p])
            copy.start()
            waits.append(copy.wait)

    outs = (qkv_out, wout_out, extra_out)
    sems = (ring_send, ring_recv, core_send, core_recv)
    waits += ring_gather(cycle, cut, 0, hops, (qkv_ref, wout_ref, extra_ref), outs, sems, (swap,))
    for wait in waits:
        wait()


def front_rest_kernel(cycle, group, fixed, cut, hops, qkv_in, wout_in, extra_in, x_ref, routes_ref, prompt_cot_ref, cont_cot_ref,
                      qkv_out, wout_out, extra_out, x_out, target_ref, cots_ref,
                      ring_send, ring_recv, core_send, core_recv, row_send, row_recv):
    own = lax.axis_index("expert")
    rows = [lax.rem(own + s, group) for s in range(1, group)]
    greet(ring_neighbours(cycle) + [{"expert": g} for g in rows])
    waits = []

    def others():
        for s, g in enumerate(rows):
            back = lax.rem(own + group - (s + 1), group)
            copy = remote(x_ref, x_out.at[s], {"expert": back}, row_send.at[s], row_recv.at[s])
            copy.start()
            waits.append(remote(x_ref, x_out.at[s], {"expert": g}, row_send.at[s], row_recv.at[s]).wait_recv)
            waits.append(copy.wait_send)
        cots_kernel(*fixed, routes_ref, (prompt_cot_ref, cont_cot_ref), target_ref, cots_ref)

    outs = (qkv_out, wout_out, extra_out)
    sems = (ring_send, ring_recv, core_send, core_recv)
    waits += ring_gather(cycle, cut, hops, len(cycle) // 2, None, outs, sems, (others,))
    for wait in waits:
        wait()


def front(w_qkv, w_out, extra, expert_in, x_prompt, routes, prompt_cot, cont_cot, fixed, cycle, group):
    count = len(cycle)
    experts, padded = fixed[2:]
    rows, columns = w_qkv.shape
    cut = (columns + w_out.shape[1] + extra.shape[1]) // 256 * 128
    hops = count // 4
    anywhere, vmem = pl.BlockSpec(memory_space=pl.ANY), pl.BlockSpec(memory_space=pltpu.VMEM)
    ring_sems = [pltpu.SemaphoreType.DMA((4, count, 4))] * 2 + [pltpu.SemaphoreType.DMA((4 * count,))] * 2
    dense_shapes = tuple(jax.ShapeDtypeStruct((count, 2) + v.shape, bf16) for v in (w_qkv, w_out, extra))
    cost = pl.CostEstimate(flops=10**10, bytes_accessed=10**8, transcendentals=0)
    *dense, w_in = pl.pallas_call(
        functools.partial(front_kernel, cycle, cut, hops),
        out_shape=dense_shapes + (jax.ShapeDtypeStruct(expert_in.shape, bf16),),
        in_specs=[anywhere] * 4,
        out_specs=(anywhere,) * 4,
        scratch_shapes=ring_sems + [pltpu.SemaphoreType.DMA((3,))] * 2 + [pltpu.SemaphoreType.DMA((4,))],
        compiler_params=pltpu.CompilerParams(collective_id=0, has_side_effects=True, vmem_limit_bytes=VMEM_LIMIT),
        cost_estimate=cost,
        name="front",
    )(w_qkv, w_out, extra, expert_in)
    results = pl.pallas_call(
        functools.partial(front_rest_kernel, cycle, group, fixed, cut, hops),
        out_shape=dense_shapes
        + (
            jax.ShapeDtypeStruct((group - 1,) + x_prompt.shape, bf16),
            jax.ShapeDtypeStruct(routes.shape, jnp.int32),
            jax.ShapeDtypeStruct((experts, padded, prompt_cot.shape[1]), bf16),
        ),
        in_specs=[anywhere] * 4 + [vmem] * 3,
        out_specs=(anywhere,) * 4 + (vmem,) * 2,
        scratch_shapes=ring_sems + [pltpu.SemaphoreType.DMA((group,))] * 2,
        input_output_aliases={0: 0, 1: 1, 2: 2},
        compiler_params=pltpu.CompilerParams(collective_id=4, has_side_effects=True, vmem_limit_bytes=VMEM_LIMIT),
        cost_estimate=cost,
        name="front_rest",
    )(*dense, x_prompt, routes, prompt_cot, cont_cot)
    return [v.reshape(count * 2 * rows, v.shape[3]) for v in results[:3]] + [w_in] + list(results[3:])


def team_ring(group):
    team, own = lax.axis_index("team"), lax.axis_index("expert")

    def peer(i):
        g, t = lax.rem(own + i // 4, group), lax.rem(team + lax.rem(i, 4), 4)
        return g * 4 + t, {"team": t, "expert": g}

    def back_from(i):
        return lax.rem(own + (group - i // 4), group) * 4 + lax.rem(team + (4 - lax.rem(i, 4)), 4)

    return own * 4 + team, peer, back_from


def expert_up_kernel(units, group, experts, padded, target_ref, gate_ref, routes_ref, z_ref, cots_ref, w_in_ref,
                     active_hbm, slope_hbm, grad_hbm, dproduced_ref, arrived_t_ref,
                     stage_ref, gate_stage, arrived_ref, gate_in, held_ref, chunk_ref, dproduced_t_ref, tile_ref, row_send, row_recv, gate_send, gate_recv, held_sem, chunk_sem, tile_sem):
    me, peer, back_from = team_ring(group)
    sources = 4 * group
    hidden = w_in_ref.shape[1]
    step = next(n for n in (512, 256, 128) if hidden % n == 0)
    greet([peer(jnp.int32(i))[1] for i in range(1, sources)])
    for unit in units:
        first, rows, slot, slots = unit
        chosen = chosen_rows(target_ref, unit, experts, padded)
        got = nn(chosen, z_ref[first : first + rows, :]).astype(bf16)
        features = []
        for c in range(2):
            left = gate_ref[c : c + 1, first : first + rows]
            for _ in range(3):
                low = left.astype(bf16).astype(f32)
                features.append(low)
                left = left - low
        features.append(routes_ref[0:1, first : first + rows].astype(f32))
        features.append(jnp.zeros_like(features[0]))
        picked = nt(jnp.concatenate(features, axis=0).astype(bf16), chosen)
        gates = [picked[3 * c : 3 * c + 1] + picked[3 * c + 1 : 3 * c + 2] + picked[3 * c + 2 : 3 * c + 3] for c in range(2)]
        for e in range(experts):
            part = slice(e * slots, (e + 1) * slots)
            stage_ref[e, slot : slot + slots, :] = got[part]
            gate = jnp.where(picked[6:7, part] == float(e), gates[0][:, part], gates[1][:, part])
            gate_stage[e, :, slot : slot + slots] = jnp.broadcast_to(gate, (8, slots))

    def sends(i, to):
        number, device = peer(i)
        return (
            remote(gate_stage.at[number], gate_in.at[to], device, gate_send.at[i], gate_recv.at[i]),
            remote(stage_ref.at[number], arrived_ref.at[to], device, row_send.at[i], row_recv.at[i]),
        )

    for i in range(1, sources):
        for copy in sends(jnp.int32(i), me):
            copy.start()
    arrived_ref[me] = stage_ref[me]
    gate_in[me] = gate_stage[me]

    def keep(number, slot):
        return pltpu.make_async_copy(chunk_ref.at[slot], slope_hbm.at[number], chunk_sem.at[slot])

    def out(number):
        return pltpu.make_async_copy(held_ref.at[number], active_hbm.at[number], held_sem.at[number])

    def source(i, carry):
        number, slot = back_from(i), lax.rem(i, 2)

        @pl.when(i > 0)
        def _():
            for copy in sends(i, number):
                copy.wait_recv()

        @pl.when(i >= 2)
        def _():
            keep(back_from(i - 2), slot).wait()

        dproduced_ref[number] = (cots_ref[number].astype(f32) * gate_in[number].T[:, 0:1]).astype(bf16)
        arrived = arrived_ref[number]
        for first in range(0, hidden, step):
            at = slice(first, first + step)
            active, slope = gelu_parts(nn(arrived, w_in_ref[:, at]))
            chunk_ref[slot, :, at] = slope.astype(bf16)
            held_ref[number, :, at] = active.astype(bf16)
        keep(number, slot).start()
        out(number).start()
        return carry

    lax.fori_loop(0, sources, source, 0)
    width = dproduced_ref.shape[2]
    dproduced_t_ref[...] = dproduced_ref[...].reshape(-1, width).T
    arrived_t_ref[...] = arrived_ref[...].reshape(-1, width).T

    def put(f):
        at = pl.ds(pl.multiple_of(f * step, step), step)
        return pltpu.make_async_copy(tile_ref.at[lax.rem(f, 2)], grad_hbm.at[at, :], tile_sem.at[lax.rem(f, 2)])

    def product(f, carry):
        @pl.when(f >= 2)
        def _():
            put(f - 2).wait()

        active = held_ref[:, :, pl.ds(pl.multiple_of(f * step, step), step)].reshape(-1, step)
        tile_ref[lax.rem(f, 2)] = nn(dproduced_t_ref[...], active).astype(bf16).T
        put(f).start()
        return carry

    steps = hidden // step
    lax.fori_loop(0, steps, product, 0)
    for f in range(max(0, steps - 2), steps):
        put(jnp.int32(f)).wait()
    for i in range(sources - 2, sources):
        keep(back_from(jnp.int32(i)), jnp.int32(i % 2)).wait()
    for i in range(sources):
        out(back_from(jnp.int32(i))).wait()
    for i in range(1, sources):
        for copy in sends(jnp.int32(i), me):
            copy.wait_send()


def expert_up(target, gates, routes, z, cots, w_in, units, group, experts, padded):
    sources = 4 * group
    width, hidden = w_in.shape
    step = next(n for n in (512, 256, 128) if hidden % n == 0)
    slots = sources * padded
    anywhere, vmem = pl.BlockSpec(memory_space=pl.ANY), pl.BlockSpec(memory_space=pltpu.VMEM)
    return pl.pallas_call(
        functools.partial(expert_up_kernel, units, group, experts, padded),
        out_shape=(
            jax.ShapeDtypeStruct((sources, padded, hidden), bf16),
            jax.ShapeDtypeStruct((sources, padded, hidden), bf16),
            jax.ShapeDtypeStruct((hidden, width), bf16),
            jax.ShapeDtypeStruct((sources, padded, width), bf16),
            jax.ShapeDtypeStruct((width, slots), bf16),
        ),
        in_specs=[vmem] * 6,
        out_specs=(anywhere,) * 3 + (vmem,) * 2,
        scratch_shapes=[
            pltpu.VMEM((experts, padded, width), bf16),
            pltpu.VMEM((experts, 8, padded), f32),
            pltpu.VMEM((sources, padded, width), bf16),
            pltpu.VMEM((sources, 8, padded), f32),
            pltpu.VMEM((sources, padded, hidden), bf16),
            pltpu.VMEM((2, padded, hidden), bf16),
            pltpu.VMEM((width, slots), bf16),
            pltpu.VMEM((2, step, width), bf16),
        ]
        + [pltpu.SemaphoreType.DMA((sources,))] * 5
        + [pltpu.SemaphoreType.DMA((2,))] * 2,
        compiler_params=pltpu.CompilerParams(collective_id=1, has_side_effects=True, vmem_limit_bytes=VMEM_LIMIT),
        cost_estimate=pl.CostEstimate(flops=6 * slots * width * hidden, bytes_accessed=10**8, transcendentals=0),
        name="expert_up",
    )(target, gates, routes, z, cots, w_in)


def expert_back_kernel(units, group, experts, padded, target_ref, dproduced_hbm, slope_hbm, active_hbm, arrived_t_ref, w_in_ref, w_down_ref,
                       grad_hbm, dz_ref, inner_ref, dbefore_ref, stage_ref, back_ref, inner_stage, inner_back, tile_ref,
                       active_ref, copy_sem, active_sem, tile_sem, row_send, row_recv, inner_send, inner_recv):
    me, peer, back_from = team_ring(group)
    sources = 4 * group
    hidden = w_in_ref.shape[1]
    tile = next(t for t in (768, 512, 256) if hidden % t == 0)

    def load(i):
        number = peer(i)[0]
        return (
            pltpu.make_async_copy(slope_hbm.at[number], dbefore_ref.at[number], copy_sem.at[0, i]),
            pltpu.make_async_copy(dproduced_hbm.at[number], stage_ref.at[number], copy_sem.at[1, i]),
        )

    def sends(i, to):
        number, device = peer(i)
        return (
            remote(inner_stage.at[number], inner_back.at[to], device, inner_send.at[i], inner_recv.at[i]),
            remote(stage_ref.at[number], back_ref.at[to], device, row_send.at[i], row_recv.at[i]),
        )

    def fetch(turn):
        slot = lax.rem(turn, 2)
        return pltpu.make_async_copy(active_hbm.at[peer(lax.rem(turn + 1, sources))[0]], active_ref.at[slot], active_sem.at[slot])

    for i in list(range(1, sources)) + [0]:
        for copy in load(jnp.int32(i)):
            copy.start()
        if i in (1, 2):
            fetch(jnp.int32(i - 1)).start()
    greet([peer(jnp.int32(i))[1] for i in range(1, sources)])

    def source(step, carry):
        i = lax.rem(step + 1, sources)
        number, slot = peer(i)[0], lax.rem(step, 2)
        for copy in load(i):
            copy.wait()
        fetch(step).wait()
        dproduced = stage_ref[number]
        inner = darrived = None
        for first in range(0, hidden, tile):
            at = slice(first, first + tile)
            dactive = nt(dproduced, w_down_ref[at, :])
            product = active_ref[slot, :, at].astype(f32) * dactive
            for lane in range(0, tile, 128):
                part = product[:, lane : lane + 128]
                inner = part if inner is None else inner + part
            dbefore = (dactive * dbefore_ref[number, :, at].astype(f32)).astype(bf16)
            dbefore_ref[number, :, at] = dbefore
            part = nt(dbefore, w_in_ref[:, at])
            darrived = part if darrived is None else darrived + part

        @pl.when(step + 2 < sources)
        def _():
            fetch(step + 2).start()

        inner_stage[number] = jnp.broadcast_to(jnp.sum(inner, axis=1, keepdims=True), (padded, 128)).T[:8]
        stage_ref[number] = darrived.astype(bf16)

        @pl.when(step + 1 < sources)
        def _():
            for copy in sends(i, me):
                copy.start()

        return carry

    lax.fori_loop(0, sources, source, 0)
    back_ref[me] = stage_ref[me]
    inner_back[me] = inner_stage[me]
    wide = next(n for n in (512, 256, 128) if hidden % n == 0)
    steps = hidden // wide

    def put(f):
        at = pl.ds(pl.multiple_of(f * wide, wide), wide)
        return pltpu.make_async_copy(tile_ref.at[lax.rem(f, 2)], grad_hbm.at[:, at], tile_sem.at[lax.rem(f, 2)])

    def product(f, carry):
        @pl.when(f >= 2)
        def _():
            put(f - 2).wait()

        dbefore = dbefore_ref[:, :, pl.ds(pl.multiple_of(f * wide, wide), wide)].reshape(-1, wide)
        tile_ref[lax.rem(f, 2)] = nn(arrived_t_ref[...], dbefore).astype(bf16)
        put(f).start()
        return carry

    lax.fori_loop(0, steps, product, 0)
    for f in range(max(0, steps - 2), steps):
        put(jnp.int32(f)).wait()
    for i in range(1, sources):
        sends(jnp.int32(i), back_from(jnp.int32(i)))[0].wait_recv()

    def hits(unit, columns, e):
        first, rows, slot, slots = unit
        numbers = lax.broadcasted_iota(jnp.int32, (rows, slots), 1) + (e * padded + slot)
        return [numbers == column for column in columns]

    for unit in units:
        first, rows, slot, slots = unit
        columns = target_columns(target_ref, unit)
        sums = [0.0, 0.0]
        for e in range(experts):
            inner = inner_back[e, 0:1, slot : slot + slots]
            for c, hit in enumerate(hits(unit, columns, e)):
                sums[c] = sums[c] + jnp.sum(jnp.where(hit, inner, 0.0), axis=1, keepdims=True)
        lanes = lax.broadcasted_iota(jnp.int32, (rows, 128), 1)
        both = jnp.where(lanes == 0, sums[0], jnp.where(lanes == 1, sums[1], 0.0))
        inner_ref[:, first : first + rows] = both.T[:8]
    for i in range(1, sources):
        sends(jnp.int32(i), back_from(jnp.int32(i)))[1].wait_recv()
    for unit in units:
        first, rows, slot, slots = unit
        columns = target_columns(target_ref, unit)
        total = None
        for e in range(experts):
            hit = hits(unit, columns, e)
            part = nn(jnp.where(hit[0] | hit[1], 1.0, 0.0).astype(bf16), back_ref[e, slot : slot + slots, :])
            total = part if total is None else total + part
        dz_ref[first : first + rows, :] = total
    for i in range(1, sources):
        for copy in sends(jnp.int32(i), me):
            copy.wait_send()


def expert_back(target, dproduced, slope, active, arrived_t, w_in, w_down, units, group, experts, padded):
    sources, mine = 4 * group, target.shape[1]
    width, hidden = w_in.shape
    anywhere, vmem = pl.BlockSpec(memory_space=pl.ANY), pl.BlockSpec(memory_space=pltpu.VMEM)
    return pl.pallas_call(
        functools.partial(expert_back_kernel, units, group, experts, padded),
        out_shape=(
            jax.ShapeDtypeStruct((width, hidden), bf16),
            jax.ShapeDtypeStruct((mine, width), f32),
            jax.ShapeDtypeStruct((8, mine), f32),
        ),
        in_specs=[vmem, anywhere, anywhere, anywhere] + [vmem] * 3,
        out_specs=(anywhere, vmem, vmem),
        scratch_shapes=[
            pltpu.VMEM((sources, padded, hidden), bf16),
            pltpu.VMEM((sources, padded, width), bf16),
            pltpu.VMEM((experts, padded, width), bf16),
            pltpu.VMEM((sources, 8, padded), f32),
            pltpu.VMEM((experts, 8, padded), f32),
            pltpu.VMEM((2, width, 512 if hidden % 512 == 0 else 256 if hidden % 256 == 0 else 128), bf16),
            pltpu.VMEM((2, padded, hidden), bf16),
            pltpu.SemaphoreType.DMA((2, sources)),
            pltpu.SemaphoreType.DMA((2,)),
            pltpu.SemaphoreType.DMA((2,)),
        ]
        + [pltpu.SemaphoreType.DMA((sources,))] * 4,
        compiler_params=pltpu.CompilerParams(collective_id=2, has_side_effects=True, vmem_limit_bytes=VMEM_LIMIT),
        cost_estimate=pl.CostEstimate(flops=6 * sources * padded * width * hidden, bytes_accessed=10**8, transcendentals=0),
        name="expert_back",
    )(target, dproduced, slope, active, arrived_t, w_in, w_down)


def mix_rows(unit, experts, padded, target_ref, gate_ref, middle_ref, back_ref, out_ref):
    first, rows, slot, slots = unit
    columns = target_columns(target_ref, unit)
    turned = gate_ref[:, first : first + rows].T
    total = middle_ref[first : first + rows, :]
    for e in range(experts):
        numbers = lax.broadcasted_iota(jnp.int32, (rows, slots), 1) + (e * padded + slot)
        weight = sum(jnp.where(numbers == columns[c], turned[:, c : c + 1], 0.0) for c in range(2))
        total = total + nn(weight.astype(bf16), back_ref[e, slot : slot + slots, :])
    out_ref[first : first + rows, :] = total.astype(bf16)


def finish_kernel(cycle, group, n_prompt, units, experts, padded, *refs):
    parts, refs = refs[:3], refs[3:]
    win_ref, gain_ref, target_ref, gate_ref = refs[:4]
    brought, refs = refs[4:10], refs[10:]
    outs, refs = refs[:3], refs[3:]
    win_out, dx_ref, mixed_ref = refs[:3]
    got, send_refs, recv_refs, rows_refs = refs[3:6], refs[6:11], refs[11:16], refs[16:19]
    away_ref, home_ref = refs[19:21]
    held, refs = refs[21:27], refs[27:]
    core_send, core_recv, ring_send, ring_recv, row_send, row_recv, team_send, team_recv, away_send, away_recv, local_sem, bring_sem = refs
    dqkv_ref, w_ref, x_ref, dmiddle_ref, middle_ref, back_ref = held
    sources = list(brought)
    sources[2] = sources[2].at[: x_ref.shape[0], :]
    bring = [pltpu.make_async_copy(src, dst, bring_sem.at[k]) for k, (src, dst) in enumerate(zip(sources, held))]
    for copy in bring:
        copy.start()
    count = len(cycle)
    chip, at, core = ring_places(cycle)
    own, team = lax.axis_index("expert"), lax.axis_index("team")
    right, left, partner = at(chip(1), core), at(chip(-1), core), {"team": team + 1 - 2 * core}
    peers = [{"expert": lax.rem(own + s, group)} for s in range(1, group)]
    mates = [team + d - 4 * ((team + d) // 4) for d in range(1, 4)]
    greet([right, left, partner] + peers + [{"team": t} for t in mates])
    started, ends = [], []

    def start(copy):
        copy.start()
        started.append(copy)

    order = []
    for hop in range(count - 1):
        for distance in (-1 - hop, 1 + hop):
            if (distance + count) % count not in order:
                order.append((distance + count) % count)
    order.append(0)

    def core_copies(number, c):
        return [
            remote(part.at[:, c, 1 - core], got[k].at[c], partner, core_send.at[k, number], core_recv.at[k, number])
            for k, part in enumerate(parts)
        ]

    for number, distance in enumerate(order):
        for copy in core_copies(number, chip(distance)):
            start(copy)
    waited = []

    def ready(distance):
        number = order.index((distance + count) % count)
        if number not in waited:
            waited.append(number)
            for copy in core_copies(number, chip(distance)):
                copy.wait_recv()
        return chip(distance)

    streams = ((0, 0, 1, right, -1), (0, 2, 1, left, 1), (0, 1, 1, right, -1), (1, 0, 1, left, 1), (2, 0, 1, left, 1))

    def hop_on(hop):
        for way, (k, lo, blocks, device, sign) in enumerate(streams):
            c = ready(sign * (1 + hop))
            for i in range(blocks):
                total = parts[k][lo + i, c, core].astype(f32) + got[k][c, lo + i].astype(f32)
                if hop:
                    if i == 0:
                        slot = recv_refs[way].at[hop - 1]
                        remote(slot, slot, device, ring_send.at[way, hop - 1], ring_recv.at[way, hop - 1]).wait_recv()
                    total = total + recv_refs[way][hop - 1, i].astype(f32)
                if hop < count - 1:
                    send_refs[way][hop, i] = total.astype(bf16)
                else:
                    rows_refs[k][own, lo + i] = total.astype(bf16)
            if hop < count - 1:
                start(remote(send_refs[way].at[hop], recv_refs[way].at[hop], device, ring_send.at[way, hop], ring_recv.at[way, hop]))

    def swap():
        for d, t in enumerate(mates):
            start(remote(win_ref.at[t], win_out.at[team], {"team": t}, team_send.at[d], team_recv.at[d]))
            source = team + 3 - d - 4 * ((team + 3 - d) // 4)
            ends.append(remote(win_ref.at[t], win_out.at[source], {"team": t}, team_send.at[d], team_recv.at[d]))
        keep = pltpu.make_async_copy(win_ref.at[team], win_out.at[team], local_sem)
        keep.start()
        keeps.append(keep)

    keeps, here = [], []

    def have(*numbers):
        for k in numbers:
            if k not in here:
                here.append(k)
                bring[k].wait()

    mine, width = dx_ref.shape
    chunk = 256 if n_prompt % 256 == 0 and mine % 256 == 0 else 128

    def front_rows(first):
        have(0, 1)
        return sum(
            nt(dqkv_ref[c, first : first + chunk, :], w_ref[:, c * width : (c + 1) * width]) for c in range(3)
        )

    def away_chunk(first):
        s, row = first // n_prompt, first % n_prompt
        away_ref[s, row : row + chunk, :] = front_rows(mine + first).astype(bf16)
        if row + chunk == n_prompt:
            start(remote(away_ref.at[s], home_ref.at[s], peers[s], away_send.at[s], away_recv.at[s]))

    def own_chunk(first):
        dx_ref[first : first + chunk, :] = front_rows(first)

    def last_chunk(first):
        have(2, 3)
        at = slice(first, first + chunk)
        x = x_ref[at, :].astype(f32)
        inverse = lax.rsqrt(jnp.mean(x * x, axis=-1, keepdims=True) + epsilon)
        unit = x * inverse
        dnormed = dx_ref[at, :]
        if first < n_prompt:
            for s in range(group - 1):
                dnormed = dnormed + home_ref[s, at, :].astype(f32)
        dunit = dnormed * gain_ref[0:1, :]
        dx_ref[at, :] = dmiddle_ref[at, :] + inverse * (dunit - unit * jnp.mean(dunit * unit, axis=-1, keepdims=True))

    fillers = [functools.partial(away_chunk, first) for first in range(0, (group - 1) * n_prompt, chunk)]
    fillers += [functools.partial(own_chunk, first) for first in range(0, mine, chunk)]

    def mix(unit):
        have(4, 5)
        mix_rows(unit, experts, padded, target_ref, gate_ref, middle_ref, back_ref, mixed_ref)

    fillers += [functools.partial(mix, unit) for unit in units]
    fillers += [functools.partial(last_chunk, first) for first in range(n_prompt, mine, chunk)]
    for hop in range(count - 1):
        hop_on(hop)
        if hop == 0:
            swap()
        for filler in fillers[hop * len(fillers) // (count - 1) : (hop + 1) * len(fillers) // (count - 1)]:
            filler()
    hop_on(count - 1)
    for s, peer in enumerate(peers):
        for k, rows in enumerate(rows_refs):
            start(remote(rows.at[own], rows.at[own], peer, row_send.at[k, s], row_recv.at[k, s]))
    for s in range(1, group):
        remote(away_ref.at[s - 1], home_ref.at[s - 1], peers[s - 1], away_send.at[s - 1], away_recv.at[s - 1]).wait_recv()
    for first in range(0, n_prompt, chunk):
        last_chunk(first)
    for s in range(1, group):
        other = lax.rem(own + group - s, group)
        for k, rows in enumerate(rows_refs):
            remote(rows.at[other], rows.at[other], peers[s - 1], row_send.at[k, s - 1], row_recv.at[k, s - 1]).wait_recv()
    for out, rows in zip(outs, rows_refs):
        for i in range(rows.shape[1]):
            total = rows[0, i].astype(f32)
            for j in range(1, group):
                total = total + rows[j, i].astype(f32)
            out[:, i * rows.shape[3] : (i + 1) * rows.shape[3]] = total
    for copy in ends:
        copy.wait_recv()
    for copy in started:
        copy.wait_send()
    for copy in keeps:
        copy.wait()


def finish(parts, grad_in, gain, target, gates, dqkv, w_qkv, x, dmiddle, middle, back, n_prompt, units, padded, cycle, group):
    count = len(cycle)
    depth = parts[0].shape[1]
    rows = depth // (2 * count)
    mine, width = dmiddle.shape
    experts = back.shape[0]
    shapes = [(v.shape[0], v.shape[2]) for v in parts]
    streams = [(1, shapes[0][1])] * 3 + [shapes[1], shapes[2]]
    anywhere, vmem = pl.BlockSpec(memory_space=pl.ANY), pl.BlockSpec(memory_space=pltpu.VMEM)
    ring = [pltpu.VMEM((count - 1, k, rows, n), bf16) for k, n in streams]
    return pl.pallas_call(
        functools.partial(finish_kernel, cycle, group, n_prompt, units, experts, padded),
        out_shape=tuple(jax.ShapeDtypeStruct((rows, k * n), f32) for k, n in shapes)
        + (
            jax.ShapeDtypeStruct(grad_in.shape, bf16),
            jax.ShapeDtypeStruct((mine, width), f32),
            jax.ShapeDtypeStruct((mine, width), bf16),
        ),
        in_specs=[vmem] * 3 + [anywhere] + [vmem] * 3 + [anywhere] * 6,
        out_specs=(vmem,) * 3 + (anywhere,) + (vmem,) * 2,
        scratch_shapes=[pltpu.VMEM((count, k, rows, n), bf16) for k, n in shapes]
        + ring
        + ring
        + [pltpu.VMEM((group, k, rows, n), bf16) for k, n in shapes]
        + [pltpu.VMEM((group - 1, n_prompt, width), bf16)] * 2
        + [
            pltpu.VMEM(dqkv.shape, bf16),
            pltpu.VMEM((depth, 3 * width), bf16),
            pltpu.VMEM((mine, width), bf16),
            pltpu.VMEM((mine, width), f32),
            pltpu.VMEM((mine, width), f32),
            pltpu.VMEM(back.shape, bf16),
        ]
        + [pltpu.SemaphoreType.DMA((3, count))] * 2
        + [pltpu.SemaphoreType.DMA((5, count))] * 2
        + [pltpu.SemaphoreType.DMA((3, group))] * 2
        + [pltpu.SemaphoreType.DMA((3,))] * 2
        + [pltpu.SemaphoreType.DMA((group,))] * 2
        + [pltpu.SemaphoreType.DMA, pltpu.SemaphoreType.DMA((6,))],
        compiler_params=pltpu.CompilerParams(collective_id=3, has_side_effects=True, vmem_limit_bytes=VMEM_LIMIT),
        cost_estimate=pl.CostEstimate(flops=3 * 10**10, bytes_accessed=10**8, transcendentals=0),
        name="finish",
    )(
        *[v.reshape(v.shape[0], count, 2, rows, v.shape[2]) for v in parts],
        grad_in,
        gain,
        target,
        gates,
        dqkv,
        w_qkv,
        x,
        dmiddle,
        middle,
        back,
    )


def scatter_expert(grad):
    return lax.psum_scatter(grad, "depth", scatter_dimension=0, tiled=True).reshape(4, -1, grad.shape[1])


def whole_kernel(kernel, out_shape, flops, name, *args):
    return pl.pallas_call(
        kernel,
        out_shape=out_shape,
        compiler_params=pltpu.CompilerParams(vmem_limit_bytes=VMEM_LIMIT),
        cost_estimate=pl.CostEstimate(flops=flops, bytes_accessed=sum(a.size * a.dtype.itemsize for a in args), transcendentals=0),
        name=name,
    )(*args)


def gelu_parts(x):
    a = 0.7978845608028654
    square = x * x
    t = jnp.tanh(x * (a + (a * 0.044715) * square))
    half = 0.5 + 0.5 * t
    return x * half, half + (0.5 * x) * (1.0 - t * t) * (a + (3 * a * 0.044715) * square)


def rms_inverse(x):
    return lax.rsqrt(jnp.mean(x * x, axis=-1, keepdims=True) + epsilon)


def rms_grad(x, inverse, gain, dnormed):
    unit = x * inverse
    dunit = dnormed * gain
    dx = inverse * (dunit - unit * jnp.mean(dunit * unit, axis=-1, keepdims=True))
    return dx, jnp.sum(dnormed * unit, axis=0)


def per_device(
    cycle,
    prompt_in,
    cont_in,
    prompt_cot,
    cont_cot,
    prompt_route,
    cont_route,
    rel_bucket,
    norm_attn,
    norm_ffn,
    w_qkv,
    w_out,
    rel_w,
    w_router,
    expert_in,
    expert_out,
):
    shard = w_qkv.shape[0]
    fsdp = lax.axis_size("depth") * lax.axis_size("team")
    group = lax.axis_size("expert")
    width = shard * fsdp
    head_count = rel_w.shape[1]
    head_size = width // head_count
    pairs = head_count // 2
    experts = w_router.shape[1]
    n_prompt, n_cont = prompt_in.shape[1], cont_in.shape[2]
    mine, prompt_len = n_prompt + n_cont, n_prompt * group
    cap_prompt = (10 * n_prompt + 4 * experts - 1) // (4 * experts)
    cap_cont = (10 * n_cont + 4 * experts - 1) // (4 * experts)
    padded = (cap_prompt + cap_cont + 15) // 16 * 16
    units = unit_list(n_prompt, n_cont, cap_prompt, cap_cont, padded)
    own = lax.axis_index("expert")
    own_list = jnp.reshape(own, (1,)).astype(jnp.int32)

    rel_rows = rel_w.shape[0] * head_count
    extra = [
        w_router,
        norm_attn[:, None],
        norm_ffn[:, None],
        jnp.pad(rel_w.reshape(-1), (0, shard - rel_rows))[:, None],
        jnp.zeros((shard, 128 - experts - 3), bf16),
    ]
    routes = jnp.concatenate([prompt_route[0], cont_route[0, 0]]).T
    routes = jnp.pad(routes, ((0, 6), (0, 0)), constant_values=-1)
    fixed = (units, ((n_prompt, cap_prompt), (n_cont, cap_cont)), experts, padded)
    qkv_full, out_full, misc, w_in, x_other, target, cot_slots = front(
        w_qkv, w_out, jnp.concatenate(extra, axis=1), expert_in, prompt_in[0], routes, prompt_cot[0], cont_cot[0, 0], fixed, cycle, group
    )
    w_in = lax.all_gather(w_in.reshape(-1, w_in.shape[2]), "depth", axis=0, tiled=True)
    expert_out, qkv_full = lax.optimization_barrier((expert_out, qkv_full))
    w_down = lax.all_to_all(expert_out, "team", split_axis=0, concat_axis=0, tiled=True)
    cots = lax.all_to_all(cot_slots, ("expert", "team"), split_axis=0, concat_axis=0, tiled=True)
    cot = jnp.concatenate([prompt_cot[0], cont_cot[0, 0]]).astype(f32)
    router_full = misc[:, :experts]
    gain_attn = misc[:, experts].astype(f32)
    gain_ffn = misc[:, experts + 1].astype(f32)
    rel_full = misc[:, experts + 2].reshape(fsdp, shard)[:, :rel_rows].reshape(-1, head_count)
    buckets = rel_full.shape[0]

    x_low = jnp.concatenate([prompt_in[0], cont_in[0, 0], x_other.reshape(-1, width)])
    x_all = x_low.astype(f32)
    x = x_all[:mine]
    bucket_hot = (rel_bucket[None, :] == jnp.arange(buckets, dtype=jnp.int32)[:, None]).astype(f32)
    dist_table = jnp.einsum("bt,bh->ht", bucket_hot, rel_full.astype(f32), precision=lax.Precision.HIGHEST)
    table = jnp.concatenate([jnp.full((head_count, prompt_len), blocked, f32), dist_table], axis=1)
    table = table.reshape(pairs, 2, -1)
    inverse_x = rms_inverse(x_all)
    normed = (x_all * inverse_x * gain_attn).astype(bf16)
    qkv = jnp.dot(normed, qkv_full, preferred_element_type=f32).astype(bf16)
    heads_out, lse = attend(own_list, table, qkv, n_prompt, n_cont, group, head_size)
    w_down, cots, heads_out = lax.optimization_barrier((w_down, cots, heads_out))
    w_down = lax.all_gather(w_down.reshape(-1, w_down.shape[2]), "depth", axis=0, tiled=True)

    middle = x + jnp.dot(heads_out, out_full, preferred_element_type=f32)
    inverse_m = rms_inverse(middle)
    normed_ffn = (middle * inverse_m * gain_ffn).astype(bf16)
    logits = lax.dot_general(router_full, normed_ffn, (((0,), (1,)), ((), ())), preferred_element_type=f32)
    hot = [(jnp.arange(experts, dtype=jnp.int32)[:, None] == routes[c : c + 1]).astype(f32) for c in range(2)]
    picked = jnp.stack([jnp.sum(logits * h, axis=0) for h in hot])
    gates = jax.nn.softmax(picked, axis=0)
    gate_rows = jnp.pad(gates, ((0, 6), (0, 0)))

    active, slope, grad_down, dproduced, arrived_t = expert_up(
        target, gate_rows, routes, normed_ffn, cots, w_in, units, group, experts, padded
    )
    sum_down = scatter_expert(grad_down)
    grad_in, dnormed, inner = expert_back(target, dproduced, slope, active, arrived_t, w_in, w_down, units, group, experts, padded)
    sum_in = scatter_expert(grad_in)
    active, inner = lax.optimization_barrier((active, inner))
    dpicked = inner[:2] - gates * jnp.sum(inner[:2], axis=0, keepdims=True)
    dlogits = hot[0] * dpicked[0] + hot[1] * dpicked[1]
    terms, left = [], dlogits
    for _ in range(3):
        terms.append(left.astype(bf16))
        left = left - terms[-1].astype(f32)
    terms = jnp.concatenate(terms)
    dnormed = dnormed + lax.dot_general(
        terms, jnp.concatenate([router_full] * 3, axis=1), (((0,), (1,)), ((), ())), preferred_element_type=f32
    )
    grad_router = lax.dot_general(normed_ffn, terms, (((0,), (1,)), ((), ())), preferred_element_type=f32)
    grad_router = jnp.sum(grad_router.reshape(width, 3, experts), axis=1)
    dmiddle_part, grad_gain_ffn = rms_grad(middle, inverse_m, gain_ffn, dnormed)
    dmiddle = cot + dmiddle_part
    dattn = dmiddle.astype(bf16)
    grad_out = lax.dot_general(heads_out, dattn, (((0,), (0,)), ((), ())), preferred_element_type=f32)
    dheads = lax.dot_general(dattn, out_full, (((1,), (1,)), ((), ())), preferred_element_type=f32).astype(bf16)

    produced = jnp.dot(active.reshape(-1, active.shape[2]), w_down, preferred_element_type=f32)
    produced = produced.astype(bf16).reshape(-1, padded, width)
    back = lax.all_to_all(produced, ("expert", "team"), split_axis=0, concat_axis=0, tiled=True)
    dheads, sum_down = lax.optimization_barrier((dheads, sum_down))
    sum_down = lax.all_to_all(sum_down, "team", split_axis=0, concat_axis=0, tiled=True)

    dqkv, drel = attend_grad(own_list, table, qkv, heads_out, dheads, lse, n_prompt, n_cont, group, head_size)
    grad_qkv = jnp.einsum("rd,cre->cde", normed, dqkv, preferred_element_type=f32).astype(bf16)
    drel = drel.reshape(head_count, -1)[:, prompt_len:]
    grad_rel = jnp.einsum("bt,ht->bh", bucket_hot, drel, precision=lax.Precision.HIGHEST)

    rel_column = jnp.pad(grad_rel.reshape(fsdp, rel_rows), ((0, 0), (0, shard - rel_rows))).reshape(width, 1)
    small = [grad_router, grad_gain_ffn[:, None], rel_column, jnp.zeros((width, 128 - experts - 2), f32)]
    small = jnp.concatenate(small, axis=1).astype(bf16)
    small, sum_down = lax.optimization_barrier((small, sum_down))
    sum_qkv, sum_out, small, sum_in, dx, mixed_out = finish(
        (grad_qkv, grad_out.astype(bf16)[None], small[None]),
        sum_in,
        jnp.broadcast_to(gain_attn[None], (8, width)),
        target,
        gate_rows,
        dqkv,
        qkv_full,
        x_low,
        dmiddle,
        middle,
        back,
        n_prompt,
        units,
        padded,
        cycle,
        group,
    )
    return (
        mixed_out[:n_prompt][None],
        mixed_out[n_prompt:][None, None],
        dx[:n_prompt][None],
        dx[n_prompt:][None, None],
        jnp.sum(sum_qkv * w_qkv.astype(f32), axis=1) / norm_attn.astype(f32),
        small[:, experts],
        sum_qkv,
        sum_out,
        small[:rel_rows, experts + 1].reshape(-1, head_count),
        small[:, :experts],
        sum_in.astype(f32),
        sum_down.astype(f32),
    )


def ring_of_chips(mesh):
    devices = mesh.devices[:, 0]
    chips = len(devices) // 2
    across = [getattr(d, "coords", None) for d in devices[::2]]
    if any(c is None for c in across):
        return list(range(chips))
    columns = len({tuple(c)[0] for c in across})
    levels = chips // columns
    if columns < 2 or levels % 2 or levels * columns != chips:
        return list(range(chips))
    cycle = [0]
    for z in range(levels):
        row = list(range(1, columns))
        cycle += [z * columns + i for i in (row if z % 2 == 0 else row[::-1])]
    return cycle + [z * columns for z in range(levels - 1, 0, -1)]


def solution(mesh):
    fsdp, group = mesh.devices.shape
    cycle = ring_of_chips(mesh)
    mesh = jax.sharding.Mesh(mesh.devices.reshape(fsdp // 4, 4, group), ("depth", "team", "expert"))
    rows = ("depth", "team")
    in_specs = (
        P(rows, "expert", None),
        P(rows, "expert", None, None),
        P(rows, "expert", None),
        P(rows, "expert", None, None),
        P(rows, "expert", None),
        P(rows, "expert", None, None),
        P(),
        P(rows),
        P(rows),
        P(rows, None),
        P(rows, None),
        P(rows, None),
        P(rows, None),
        P("expert", rows, None),
        P("expert", rows, None),
    )
    out_specs = (
        P(rows, "expert", None),
        P(rows, "expert", None, None),
        P(rows, "expert", None),
        P(rows, "expert", None, None),
        P(rows),
        P(rows),
        P(rows, None),
        P(rows, None),
        P(rows, None),
        P(rows, None),
        P("expert", rows, None),
        P("expert", rows, None),
    )
    return jax.shard_map(
        functools.partial(per_device, cycle),
        mesh=mesh,
        in_specs=in_specs,
        out_specs=out_specs,
        check_vma=False,
    )
```

profile of v0, /device:TPU:0, one launch (start us, length us, event | category | flops | bytes accessed | tf_op | source)
XLA Modules:
  0.0 518.3 jit_solution(4877262335833768049)
XLA Ops:
  7.2 0.7 reshape.130
  8.1 0.8 copy.52
  8.8 0.8 copy.50
  9.6 0.8 copy.51
  10.4 0.7 concatenate.25.extra_ref
  11.1 35.6 %front.1 = (bf16[8,2,48,2304]{3,2,1,0:T(8,128)(2,1)}, bf16[8,2,48,768]{3,2,1,0:T(8,128)(2,1)}, bf16[8,2,48,128]{3,2,1,0:T(8,128)(2,1)}, bf16[4,48,3072]{2,1,0:T(8,128)(2,1)}) custom-call(bf16[48,2304]{1,0:T(8,128)(2,1)} %qkv_ref.1, bf16[48,768]{1,0:T(8,128)(2,1)} %wout_ref.1, bf16[48,128]{1,0:T(8,128)(2,1)} %concatenate.25.extra_ref, ...), custom_call_target="tpu_custom_call" | custom-call | flops 10000000000 | bytes 100000000 | tf_op jit(solution)/shard_map/front/pallas_call | solution.py:445
  46.7 0.6 pad.19.routes_ref
  47.3 27.0 %front_rest.1 = (bf16[8,2,48,2304]{3,2,1,0:T(8,128)(2,1)}, bf16[8,2,48,768]{3,2,1,0:T(8,128)(2,1)}, bf16[8,2,48,128]{3,2,1,0:T(8,128)(2,1)}, bf16[1,512,768]{2,1...) custom-call(bf16[8,2,48,2304]{3,2,1,0:T(8,128)(2,1)} %get-tuple-elem, ...), custom_call_target="tpu_custom_call", output_to_operand_aliasing={{0}: (0, {}), {1}: (1, {}), {2}: (2, {})} | custom-call | flops 10000000000 | bytes 100000000 | tf_op jit(solution)/shard_map/front_rest/pallas_call | solution.py:455
  74.3 4.4 all-to-all-start
  78.8 1.4 fusion.22
  80.4 0.8 fusion.4
  81.2 4.0 fusion.21
  85.2 0.5 multiply_reduce_fusion
  85.7 9.0 %all-to-all-done = bf16[4,192,768]{2,1,0:T(8,128)(2,1)} async-done(((bf16[4,192,768]{2,1,0:T(8,128)(2,1)}), bf16[4,192,768]{2,1,0:T(8,128)(2,1)}, u32[]{:S(2)}, u32[]{:S(2)}) %all-to-all-start) | async-done | bytes 1179680 | tf_op jit(solution)/shard_map/all_to_all | solution.py:1098
  94.7 4.7 all-to-all-start.1
  99.4 0.3 all-gather.5.cloned.1.call-start
  99.7 0.1 copy.69
  99.8 0.7 reshape.133.table_ref
  100.6 10.1 %convolution_convert_fusion.q_ref.k_ref.v_ref = bf16[1536,2304]{1,0:T(8,128)(2,1)} fusion(bf16[768,2304]{1,0:T(8,128)(2,1)} %bitcast.99, f32[768]{0:T(1024)S(1)} %convert_reduce_fusion.1, f32[1536]{0:T(1024)S(1)} %add_rsqrt_fusion, bf16[1536,768]{1,0:T(8,128)(2,1)S(1)} %get-tuple-element.131.refs_9_), kind=kOutput, calls=%fused_computation | convolution fusion | flops 5444075520 | bytes 12985344 | tf_op jit(solution)/shard_map/dot_general | solution.py:1116
  110.6 36.0 %attend.1 = (bf16[1024,768]{1,0:T(8,128)(2,1)}, f32[6,2,1024]{2,1,0:T(2,128)}) custom-call(s32[1]{0:T(128)} %bitcast.own_ref, f32[6,2,2560]{2,1,0:T(2,128)} %reshape.133.table_ref, bf16[1536,2304]{1,0:T(8,128)(2,1)} %convolution_convert_fusion.q_ref.k_ref.v_ref, bf16[1536,2304]{1,0:T(8,128)(2,1)} %convolution_convert_fusion.q_ref.k_ref.v_ref, ...), custom_call_target="tpu_custom_call" | custom-call | flops 16106127360 | bytes 12582912 | tf_op jit(solution)/shard_map/attend/pallas_call | solution.py:163
  146.6 0.4 reduce-scatter.3.cloned.1.call-start
  147.2 4.2 multiply_reduce_fusion.3
  151.4 0.3 multiply_convert_fusion.1.z_ref
  151.8 1.4 copy-done.1
  153.1 0.5 select_reduce_fusion
  153.8 0.6 pad.20.gate_ref.refs_6_
  154.4 74.6 %expert_up.1 = (bf16[8,320,3072]{2,1,0:T(8,128)(2,1)}, bf16[8,320,3072]{2,1,0:T(8,128)(2,1)}, bf16[3072,768]{1,0:T(8,128)(2,1)}, bf16[8,320,768]{2,1,0:T(8,128)(2,1)}, bf16[768,2560]{1,0:T(8,128)(2,1)}) custom-call(s32[8,1024]{1,0:T(8,128)} %get-tuple-element.63.target_ref.refs_5_, f32[8,1024]{1,0:T(8,128)} %pad.20.gate_ref.refs_6_, ...), custom_call_target="tpu_custom_call" | custom-call | flops 36238786560 | bytes 100000000 | tf_op jit(solution)/shard_map/expert_up/pallas_call | solution.py:596
  229.0 10.7 %reduce-scatter.5.cloned.1.call-start = ((), (), s32[]{:S(2)}) async-start(), calls=%async_computation.9 | async-start | bytes 5898240 | tf_op jit(solution)/shard_map/reduce_scatter | solution.py:1015
  239.9 80.9 %expert_back.1 = (bf16[768,3072]{1,0:T(8,128)(2,1)}, f32[1024,768]{1,0:T(8,128)}, f32[8,1024]{1,0:T(8,128)}) custom-call(s32[8,1024]{1,0:T(8,128)} %get-tuple-element.63.target_ref.refs_5_, bf16[8,320,768]{2,1,0:T(8,128)(2,1)} %get-tuple-element.66.dproduced_hbm, bf16[8,320,3072]{2,1,0:T(8,128)(2,1)} %get-tuple-element.67.slope_hbm, ...), custom_call_target="tpu_custom_call" | custom-call | flops 36238786560 | bytes 100000000 | tf_op jit(solution)/shard_map/expert_back/pallas_call | solution.py:754
  320.8 0.8 slice_reduce_fusion.3
  321.6 0.8 multiply_subtract_fusion
  322.4 4.5 multiply_reduce_fusion.1
  327.0 3.2 multiply_add_fusion.refs_10_
  330.2 1.7 copy-done.9
  331.9 2.6 convolution_convert_fusion.3.do_ref
  334.5 3.9 all-to-all-start.2
  338.4 17.8 %convolution_convert_fusion.1 = bf16[2560,768]{1,0:T(8,128)(2,1)} fusion(bf16[2560,3072]{1,0:T(8,128)(2,1)} %bitcast.97, bf16[3072,768]{1,0:T(8,128)(2,1)} %all-gather.5.cloned.1.call-done.w_down_ref), kind=kOutput, calls=%fused_computation.1 | convolution fusion | flops 12081561600 | bytes 24379392 | tf_op jit(solution)/shard_map/dot_general | solution.py:1155
  356.2 0.3 fusion.1
  356.6 0.2 copy.61
  356.8 0.2 broadcast_in_dim.62
  356.9 4.9 convolution_convert_fusion.4
  361.9 1.0 copy-done.6
  362.9 4.5 all-to-all-start.3
  367.5 49.9 %attend_grad.1 = (bf16[3,1536,768]{2,1,0:T(8,128)(2,1)}, f32[6,2,2560]{2,1,0:T(2,128)}) custom-call(s32[1]{0:T(128)} %bitcast.own_ref, f32[6,2,2560]{2,1,0:T(2,128)} %reshape.133.table_ref, bf16[1536,2304]{1,0:T(8,128)(2,1)} %convolution_convert_fusion.q_ref.k_ref.v_ref, bf16[1536,2304]{1,0:T(8,128)(2,1)} %convolution_convert_fusion.q_ref.k_ref.v_ref, ...), custom_call_target="tpu_custom_call" | custom-call | flops 40265318400 | bytes 31457280 | tf_op jit(solution)/shard_map/attend_grad/pallas_call | solution.py:189
  417.4 1.0 reshape.142
  418.4 0.2 convolution_convert_fusion.5
  418.5 0.1 copy.60
  418.8 0.2 reshape.151
  419.0 0.9 maximum_maximum_fusion
  419.9 10.7 %convolution_convert_fusion.2 = bf16[3,768,768]{1,2,0:T(8,128)(2,1)} fusion(bf16[3,1536,768]{2,1,0:T(8,128)(2,1)} %get-tuple-element.77.refs_7_, f32[768]{0:T(1024)S(1)} %copy-done.19, f32[1536]{0:T(1024)S(1)} %copy-done.21, bf16[1536,768]{1,0:T(8,128)(2,1)S(1)} %copy-done.4), kind=kOutput, calls=%fused_computation.10 | convolution fusion | flops 5442306048 | bytes 12985344 | tf_op jit(solution)/shard_map/rd,cre->cde/dot_general | solution.py:1162
  430.6 1.6 convert_element_type.114
  432.2 0.6 broadcast_in_dim.57.refs_4_
  432.8 64.4 %finish.1 = (f32[48,2304]{1,0:T(8,128)}, f32[48,768]{1,0:T(8,128)}, f32[48,128]{1,0:T(8,128)}, bf16[4,48,3072]{2,1,0:T(8,128)(2,1)}, f32[1024,768]{1,0:T(8,128)}, /*index=5*/bf16[1024,768]{1,0:T(8,128)(2,1)}) custom-call(bf16[3,8,2,48,768]{4,3,2,1,0:T(8,128)(2,1)} %bitcast.98, bf16[1,8,2,48,768]{4,3,2,1,0:T(8,128)(2,1)} %bitcast.101, ...), custom_call_target="tpu_custom_call" | custom-call | flops 30000001024 | bytes 100000000 | tf_op jit(solution)/shard_map/finish/pallas_call | solution.py:967
  497.2 1.2 multiply_reduce_fusion.4
  498.4 0.9 slice_reduce_fusion.2
  499.3 1.4 slice_reduce_fusion.1
  500.7 2.8 slice_bitcast_fusion.2
  503.5 0.5 convert_divide_fusion
  504.0 0.6 reshape_squeeze.7
  504.7 0.7 copy.64
  505.3 2.9 convert_element_type.113
  508.3 1.9 slice_bitcast_fusion
  510.1 0.8 copy.78
  510.9 0.7 copy.79
  (85 shorter events, 1.1 us)
Async XLA Ops:
  7.2 147.2 %all-gather.3.cloned.1.call-start = ((), (), s32[]{:S(2)}) async-start(), calls=%async_computation.6 | async-start | bytes 5898240 | tf_op jit(solution)/shard_map/all_gather | solution.py:1096
  11.1 35.6 %copy-start.22 = (s32[1,1,512,2]{2,3,1,0:T(2,128)S(1)}, s32[1,1,512,2]{2,3,1,0:T(2,128)}, u32[]{:S(2)}) copy-start(s32[1,1,512,2]{2,3,1,0:T(2,128)} %param.20) | copy-start | bytes 12292
  11.1 35.6 %copy-start.23 = (s32[1,512,2]{1,2,0:T(2,128)S(1)}, s32[1,512,2]{1,2,0:T(2,128)}, u32[]{:S(2)}) copy-start(s32[1,512,2]{1,2,0:T(2,128)} %param.19) | copy-start | bytes 12292
  74.3 6.0 %copy-start.16 = (s32[1536]{0:T(1024)S(1)}, s32[1536]{0:T(1024)}, u32[]{:S(2)}) copy-start(s32[1536]{0:T(1024)} %param.21) | copy-start | bytes 18436
  74.3 6.9 %copy-start.11 = (bf16[1,512,768]{2,1,0:T(8,128)(2,1)S(1)}, bf16[1,512,768]{2,1,0:T(8,128)(2,1)}, u32[]{:S(2)}) copy-start(bf16[1,512,768]{2,1,0:T(8,128)(2,1)} %param.15) | copy-start | bytes 2359300
  74.3 20.3 %all-to-all-start = ((bf16[4,192,768]{2,1,0:T(8,128)(2,1)}), bf16[4,192,768]{2,1,0:T(8,128)(2,1)}, u32[]{:S(2)}, u32[]{:S(2)}) async-start(bf16[4,192,768]{2,1,0:T(8,128)(2,1)} %param.29), calls=%async_computation | async-start | bytes 2359296 | tf_op jit(solution)/shard_map/all_to_all | solution.py:1098
  85.2 15.4 %copy-start.3 = (bf16[1536,768]{1,0:T(8,128)(2,1)}, bf16[1536,768]{1,0:T(8,128)(2,1)S(1)}, u32[]{:S(2)}) copy-start(bf16[1536,768]{1,0:T(8,128)(2,1)S(1)} %get-tuple-element.131.refs_9_) | copy-start | bytes 7077892
  94.7 5.1 copy-start.12
  94.7 51.9 %all-to-all-start.1 = ((bf16[8,320,768]{2,1,0:T(8,128)(2,1)}), bf16[8,320,768]{2,1,0:T(8,128)(2,1)}, u32[]{:S(2)}, u32[]{:S(2)}) async-start(bf16[8,320,768]{2,1,0:T(8,128)(2,1)} %get-tuple-element.59), calls=%async_computation.1 | async-start | bytes 7864320 | tf_op jit(solution)/shard_map/all_to_all | solution.py:1099
  99.4 140.5 %all-gather.5.cloned.1.call-start = ((), (), s32[]{:S(2)}) async-start(), calls=%async_computation.7 | async-start | bytes 5898240 | tf_op jit(solution)/shard_map/all_gather | solution.py:1119
  99.6 11.0 %copy-start.20 = (f32[1536]{0:T(1024)}, f32[1536]{0:T(1024)S(1)}, u32[]{:S(2)}) copy-start(f32[1536]{0:T(1024)S(1)} %add_rsqrt_fusion) | copy-start | bytes 18436
  100.6 10.1 %copy-start.18 = (f32[768]{0:T(1024)}, f32[768]{0:T(1024)S(1)}, u32[]{:S(2)}) copy-start(f32[768]{0:T(1024)S(1)} %convert_reduce_fusion.1) | copy-start | bytes 9220
  146.6 187.8 %reduce-scatter.3.cloned.1.call-start = ((), (), s32[]{:S(2)}) async-start(), calls=%async_computation.8 | async-start | bytes 5898240 | tf_op jit(solution)/shard_map/reduce_scatter | solution.py:1015
  151.4 175.6 %copy-start = (f32[1024,768]{1,0:T(8,128)}, f32[1024,768]{1,0:T(8,128)S(1)}, u32[]{:S(2)}) copy-start(f32[1024,768]{1,0:T(8,128)S(1)} %get-tuple-element.147.refs_11_) | copy-start | bytes 9437188
  151.4 1.8 copy-start.5
  151.7 1.4 copy-start.1
  229.0 203.2 %reduce-scatter.5.cloned.1.call-start = ((), (), s32[]{:S(2)}) async-start(), calls=%async_computation.9 | async-start | bytes 5898240 | tf_op jit(solution)/shard_map/reduce_scatter | solution.py:1015
  327.0 4.9 copy-start.25
  330.2 1.7 copy-start.9
  334.5 27.4 %all-to-all-start.2 = ((bf16[4,192,768]{2,1,0:T(8,128)(2,1)}), bf16[4,192,768]{2,1,0:T(8,128)(2,1)S(1)}, u32[]{:S(2)}, u32[]{:S(2)}) async-start(bf16[4,192,768]{2,1,0:T(8,128)(2,1)} %bitcast.68), calls=%async_computation.3 | async-start | bytes 2359296 | tf_op jit(solution)/shard_map/all_to_all | solution.py:1159
  338.4 17.8 %copy-start.2 = (bf16[1024,768]{1,0:T(8,128)(2,1)S(1)}, bf16[1024,768]{1,0:T(8,128)(2,1)}, u32[]{:S(2)}) copy-start(bf16[1024,768]{1,0:T(8,128)(2,1)} %copy-done.1) | copy-start | bytes 4718596
  361.9 1.0 copy-start.6
  362.9 69.3 %all-to-all-start.3 = ((bf16[8,320,768]{2,1,0:T(8,128)(2,1)}), bf16[8,320,768]{2,1,0:T(8,128)(2,1)}, u32[]{:S(2)}, u32[]{:S(2)}) async-start(bf16[8,320,768]{2,1,0:T(8,128)(2,1)} %bitcast.66), calls=%async_computation.5 | async-start | bytes 7864320 | tf_op jit(solution)/shard_map/all_to_all | solution.py:1157
  367.5 50.9 %copy-start.17 = (s32[1536]{0:T(1024)S(1)}, s32[1536]{0:T(1024)}, u32[]{:S(2)}) copy-start(s32[1536]{0:T(1024)} %param.21) | copy-start | bytes 18436
  367.5 52.4 %copy-start.4 = (bf16[1536,768]{1,0:T(8,128)(2,1)S(1)}, bf16[1536,768]{1,0:T(8,128)(2,1)}, u32[]{:S(2)}) copy-start(bf16[1536,768]{1,0:T(8,128)(2,1)} %copy-done.3) | copy-start | bytes 7077892
  367.5 52.4 %copy-start.19 = (f32[768]{0:T(1024)S(1)}, f32[768]{0:T(1024)}, u32[]{:S(2)}) copy-start(f32[768]{0:T(1024)} %copy-done.18) | copy-start | bytes 9220
  367.5 52.4 %copy-start.21 = (f32[1536]{0:T(1024)S(1)}, f32[1536]{0:T(1024)}, u32[]{:S(2)}) copy-start(f32[1536]{0:T(1024)} %copy-done.20) | copy-start | bytes 18436
  419.9 10.7 %copy-start.7 = (bf16[4,192,768]{2,1,0:T(8,128)(2,1)S(1)}, bf16[4,192,768]{2,1,0:T(8,128)(2,1)}, u32[]{:S(2)}) copy-start(bf16[4,192,768]{2,1,0:T(8,128)(2,1)} %copy-done.6) | copy-start | bytes 3538948
  432.8 64.4 %copy-start.13 = (bf16[48,2304]{1,0:T(8,128)(2,1)S(1)}, bf16[48,2304]{1,0:T(8,128)(2,1)}, u32[]{:S(2)}) copy-start(bf16[48,2304]{1,0:T(8,128)(2,1)} %qkv_ref.1) | copy-start | bytes 663556
  497.2 6.3 %copy-start.24 = (bf16[48]{0:T(256)(128)(2,1)S(1)}, bf16[48]{0:T(256)(128)(2,1)}, u32[]{:S(2)}) copy-start(bf16[48]{0:T(256)(128)(2,1)} %param.22) | copy-start | bytes 292
  497.2 7.4 %copy-start.14 = (f32[48,128]{1,0:T(8,128)S(1)}, f32[48,128]{1,0:T(8,128)}, u32[]{:S(2)}) copy-start(f32[48,128]{1,0:T(8,128)} %get-tuple-element.86) | copy-start | bytes 73732
  500.7 7.5 %copy-start.8 = (f32[1024,768]{1,0:T(8,128)S(1)}, f32[1024,768]{1,0:T(8,128)}, u32[]{:S(2)}) copy-start(f32[1024,768]{1,0:T(8,128)} %get-tuple-element.84) | copy-start | bytes 9437188
  508.3 1.9 copy-start.10
  508.3 2.6 copy-start.15
Sparse Core Ops, SparseCore 0:
  46.8 93.0 all-gather.2
  146.7 92.6 all-gather.4
  241.8 83.6 reduce-scatter.2
  327.7 86.8 reduce-scatter.4
where the time goes:
time: 521 us; the launch traced here: 518 us
  Pallas kernels  368 us (71%)
  matrix products  56.7 us (11%)
  starting transfers between devices  28.9 us (6%)
  local copies, waits for them, and re-layouts  24.2 us (5%)
  other arithmetic  16.9 us (3%)
  between operations  14.5 us (3%)
  waiting for transfers between devices  9.05 us (2%)
    pallas_call x1, Pallas kernels, expert_back(): pl.pallas_call(functools.partial(expert_back_kernel, units, group, expert...  80.9 us
    pallas_call x1, Pallas kernels, expert_up(): pl.pallas_call(functools.partial(expert_up_kernel, units, group, experts,...  74.6 us
    pallas_call x1, Pallas kernels, finish(): pl.pallas_call(functools.partial(finish_kernel, cycle, group, n_prompt, u...  64.4 us
    pallas_call x1, Pallas kernels, attend_grad(): pl.pallas_call(functools.partial(attend_grad_kernel, n_prompt, n_cont, gr...  49.9 us
    pallas_call x1, Pallas kernels, attend(): pl.pallas_call(functools.partial(attend_kernel, n_prompt, n_cont, group,...  36 us
    pallas_call x1, Pallas kernels, front(): pl.pallas_call(functools.partial(front_kernel, cycle, cut, hops), out_sha...  35.6 us
    pallas_call x1, Pallas kernels, front(): pl.pallas_call(functools.partial(front_rest_kernel, cycle, group, fixed,...  27 us
    dot_general x1, matrix products, per_device(): jnp.dot(active.reshape(-1, active.shape[2]), w_down, preferred_element_ty...  17.8 us
  transfers between devices with their start and end apart: 8, of which 1 were waited for; matrix products, arithmetic and copies ran while one was open for 14% of the time, Pallas kernels for 52%

commit v1 on v0

--- a/solution.py
+++ b/solution.py
@@ -61,9 +61,9 @@
     return parts[0] if len(parts) == 1 else jnp.concatenate(parts, axis=0)
 
 
-def head_lanes(x, h, head_size):
+def head_lanes(x, h, head_size, other=0.0):
     lanes = lax.broadcasted_iota(jnp.int32, x.shape, 1)
-    return jnp.where((lanes >= h * head_size) & (lanes < (h + 1) * head_size), x, jnp.zeros_like(x))
+    return jnp.where((lanes >= h * head_size) & (lanes < (h + 1) * head_size), x, jnp.full_like(x, other))
 
 
 def attend_kernel(n_prompt, n_cont, group, head_size, own_ref, table_ref, q_ref, k_ref, v_ref, o_ref, lse_ref, strip_ref):
@@ -80,8 +80,9 @@
                 top = jnp.max(s, axis=0, keepdims=True)
                 m_new = top if m is None else jnp.maximum(m, top)
                 p = jnp.exp(s - m_new)
-                total = jnp.sum(p, axis=0, keepdims=True)
-                out = tn(v_ref[start : start + count, :], p.astype(bf16))[h * head_size : (h + 1) * head_size]
+                both = tn(head_lanes(v_ref[start : start + count, :], h, head_size, 1.0), p.astype(bf16))
+                out = both[h * head_size : (h + 1) * head_size]
+                total = both[(1 - h) * head_size : (1 - h) * head_size + 1]
                 if m is None:
                     l, acc = total, out
                 else:
@@ -91,6 +92,24 @@
             heads.append(acc / l)
             lse_ref[0, h : h + 1, first : first + rows] = m + jnp.log(l)
         o_ref[first : first + rows, :] = jnp.concatenate(heads, axis=0).T.astype(bf16)
+
+
+def spare_lanes(row, h, head_size):
+    terms, left = [], -row
+    for _ in range(3):
+        terms.append(left.astype(bf16).astype(f32))
+        left = left - terms[-1]
+    terms.append(jnp.zeros((5, row.shape[1]), f32))
+    before = (1 - h) * head_size
+    if before:
+        terms = [jnp.zeros((before, row.shape[1]), f32)] + terms
+    terms.append(jnp.zeros((2 * head_size - before - 8, row.shape[1]), f32))
+    return jnp.concatenate(terms, axis=0).T.astype(bf16)
+
+
+def spare_ones(x, h, head_size):
+    lanes = lax.broadcasted_iota(jnp.int32, x.shape, 1) - (1 - h) * head_size
+    return jnp.where((lanes >= 0) & (lanes < 3), jnp.ones_like(x), x)
 
 
 def attend_grad_kernel(n_prompt, n_cont, group, head_size, own_ref, table_ref, q_ref, k_ref, v_ref, o_ref, do_ref, lse_ref,
@@ -111,14 +130,14 @@
             q = head_lanes(q_pair, h, head_size)
             do = head_lanes(do_pair, h, head_size)
             delta = jnp.sum(inner[h * head_size : (h + 1) * head_size], axis=0, keepdims=True)
-            lse = lse_ref[0, h : h + 1, first : first + rows]
+            q_less = q + spare_lanes(lse_ref[0, h : h + 1, first : first + rows], h, head_size)
+            do_less = do + spare_lanes(delta, h, head_size)
             dq = None
             for start, count, offset in keys:
                 at = slice(start, start + count)
                 k = k_ref[at, :]
-                s = nt(k, q) + strip_window(strip_ref, h, offset, count, rows)
-                p = jnp.exp(s - lse)
-                ds = p * (nt(v_ref[at, :], do) - delta)
+                p = jnp.exp(nt(spare_ones(k, h, head_size), q_less) + strip_window(strip_ref, h, offset, count, rows))
+                ds = p * nt(spare_ones(v_ref[at, :], h, head_size), do_less)
                 for kb in range(count // KB):
                     lane = offset - kb * KB
                     if not isinstance(lane, int):
@@ -408,15 +427,25 @@
         wait()
 
 
-def front_rest_kernel(cycle, group, fixed, cut, hops, qkv_in, wout_in, extra_in, x_ref, routes_ref, prompt_cot_ref, cont_cot_ref,
-                      qkv_out, wout_out, extra_out, x_out, target_ref, cots_ref,
-                      ring_send, ring_recv, core_send, core_recv, row_send, row_recv):
-    own = lax.axis_index("expert")
+def front_rest_kernel(cycle, group, fixed, cut, hops, qkv_in, wout_in, extra_in, wdown_ref, x_ref, routes_ref, prompt_cot_ref,
+                      cont_cot_ref, qkv_out, wout_out, extra_out, wdown_out, x_out, target_ref, cots_ref,
+                      ring_send, ring_recv, core_send, core_recv, row_send, row_recv, team_send, team_recv, local_sem):
+    own, team = lax.axis_index("expert"), lax.axis_index("team")
     rows = [lax.rem(own + s, group) for s in range(1, group)]
-    greet(ring_neighbours(cycle) + [{"expert": g} for g in rows])
+    mates = [team + d - 4 * ((team + d) // 4) for d in range(1, 4)]
+    greet(ring_neighbours(cycle) + [{"expert": g} for g in rows] + [{"team": t} for t in mates])
     waits = []
 
     def others():
+        for d, t in enumerate(mates):
+            copy = remote(wdown_ref.at[t], wdown_out.at[team], {"team": t}, team_send.at[d], team_recv.at[d])
+            copy.start()
+            source = team + 3 - d - 4 * ((team + 3 - d) // 4)
+            waits.append(remote(wdown_ref.at[t], wdown_out.at[source], {"team": t}, team_send.at[d], team_recv.at[d]).wait_recv)
+            waits.append(copy.wait_send)
+        copy = pltpu.make_async_copy(wdown_ref.at[team], wdown_out.at[team], local_sem)
+        copy.start()
+        waits.append(copy.wait)
         for s, g in enumerate(rows):
             back = lax.rem(own + group - (s + 1), group)
             copy = remote(x_ref, x_out.at[s], {"expert": back}, row_send.at[s], row_recv.at[s])
@@ -432,12 +461,12 @@
         wait()
 
 
-def front(w_qkv, w_out, extra, expert_in, x_prompt, routes, prompt_cot, cont_cot, fixed, cycle, group):
+def front(w_qkv, w_out, extra, expert_in, expert_out, x_prompt, routes, prompt_cot, cont_cot, fixed, cycle, group):
     count = len(cycle)
     experts, padded = fixed[2:]
     rows, columns = w_qkv.shape
     cut = (columns + w_out.shape[1] + extra.shape[1]) // 256 * 128
-    hops = count // 4
+    hops = max(1, count // 8)
     anywhere, vmem = pl.BlockSpec(memory_space=pl.ANY), pl.BlockSpec(memory_space=pltpu.VMEM)
     ring_sems = [pltpu.SemaphoreType.DMA((4, count, 4))] * 2 + [pltpu.SemaphoreType.DMA((4 * count,))] * 2
     dense_shapes = tuple(jax.ShapeDtypeStruct((count, 2) + v.shape, bf16) for v in (w_qkv, w_out, extra))
@@ -456,18 +485,22 @@
         functools.partial(front_rest_kernel, cycle, group, fixed, cut, hops),
         out_shape=dense_shapes
         + (
+            jax.ShapeDtypeStruct(expert_out.shape, bf16),
             jax.ShapeDtypeStruct((group - 1,) + x_prompt.shape, bf16),
             jax.ShapeDtypeStruct(routes.shape, jnp.int32),
             jax.ShapeDtypeStruct((experts, padded, prompt_cot.shape[1]), bf16),
         ),
-        in_specs=[anywhere] * 4 + [vmem] * 3,
-        out_specs=(anywhere,) * 4 + (vmem,) * 2,
-        scratch_shapes=ring_sems + [pltpu.SemaphoreType.DMA((group,))] * 2,
+        in_specs=[anywhere] * 5 + [vmem] * 3,
+        out_specs=(anywhere,) * 5 + (vmem,) * 2,
+        scratch_shapes=ring_sems
+        + [pltpu.SemaphoreType.DMA((group,))] * 2
+        + [pltpu.SemaphoreType.DMA((3,))] * 2
+        + [pltpu.SemaphoreType.DMA],
         input_output_aliases={0: 0, 1: 1, 2: 2},
         compiler_params=pltpu.CompilerParams(collective_id=4, has_side_effects=True, vmem_limit_bytes=VMEM_LIMIT),
         cost_estimate=cost,
         name="front_rest",
-    )(*dense, x_prompt, routes, prompt_cot, cont_cot)
+    )(*dense, expert_out, x_prompt, routes, prompt_cot, cont_cot)
     return [v.reshape(count * 2 * rows, v.shape[3]) for v in results[:3]] + [w_in] + list(results[3:])
 
 
@@ -628,7 +661,7 @@
     me, peer, back_from = team_ring(group)
     sources = 4 * group
     hidden = w_in_ref.shape[1]
-    tile = next(t for t in (768, 512, 256) if hidden % t == 0)
+    tile = next(t for t in (512, 256) if hidden % t == 0)
 
     def load(i):
         number = peer(i)[0]
@@ -644,52 +677,70 @@
             remote(stage_ref.at[number], back_ref.at[to], device, row_send.at[i], row_recv.at[i]),
         )
 
+    turns = sources // 2
+
+    def pair(turn):
+        return 2 * turn + 1, lax.rem(2 * turn + 2, sources)
+
     def fetch(turn):
-        slot = lax.rem(turn, 2)
-        return pltpu.make_async_copy(active_hbm.at[peer(lax.rem(turn + 1, sources))[0]], active_ref.at[slot], active_sem.at[slot])
+        return [
+            pltpu.make_async_copy(active_hbm.at[peer(i)[0]], active_ref.at[k], active_sem.at[k]) for k, i in enumerate(pair(turn))
+        ]
 
     for i in list(range(1, sources)) + [0]:
         for copy in load(jnp.int32(i)):
             copy.start()
-        if i in (1, 2):
-            fetch(jnp.int32(i - 1)).start()
+        if i == 2:
+            for copy in fetch(jnp.int32(0)):
+                copy.start()
     greet([peer(jnp.int32(i))[1] for i in range(1, sources)])
 
-    def source(step, carry):
-        i = lax.rem(step + 1, sources)
-        number, slot = peer(i)[0], lax.rem(step, 2)
-        for copy in load(i):
+    def source(turn, carry):
+        both = pair(turn)
+        numbers = [peer(i)[0] for i in both]
+        for i in both:
+            for copy in load(i):
+                copy.wait()
+        for copy in fetch(turn):
             copy.wait()
-        fetch(step).wait()
-        dproduced = stage_ref[number]
+        dproduced = jnp.concatenate([stage_ref[n] for n in numbers], axis=0)
         inner = darrived = None
         for first in range(0, hidden, tile):
             at = slice(first, first + tile)
             dactive = nt(dproduced, w_down_ref[at, :])
-            product = active_ref[slot, :, at].astype(f32) * dactive
+            active = active_ref[:, :, at].reshape(2 * padded, tile)
+            product = active.astype(f32) * dactive
             for lane in range(0, tile, 128):
                 part = product[:, lane : lane + 128]
                 inner = part if inner is None else inner + part
-            dbefore = (dactive * dbefore_ref[number, :, at].astype(f32)).astype(bf16)
-            dbefore_ref[number, :, at] = dbefore
+            slope = jnp.concatenate([dbefore_ref[n, :, at] for n in numbers], axis=0)
+            dbefore = (dactive * slope.astype(f32)).astype(bf16)
+            for k, n in enumerate(numbers):
+                dbefore_ref[n, :, at] = dbefore[k * padded : (k + 1) * padded]
             part = nt(dbefore, w_in_ref[:, at])
             darrived = part if darrived is None else darrived + part
 
-        @pl.when(step + 2 < sources)
+        @pl.when(turn + 1 < turns)
         def _():
-            fetch(step + 2).start()
-
-        inner_stage[number] = jnp.broadcast_to(jnp.sum(inner, axis=1, keepdims=True), (padded, 128)).T[:8]
-        stage_ref[number] = darrived.astype(bf16)
-
-        @pl.when(step + 1 < sources)
+            for copy in fetch(turn + 1):
+                copy.start()
+
+        inner = jnp.sum(inner, axis=1, keepdims=True)
+        for k, n in enumerate(numbers):
+            part = slice(k * padded, (k + 1) * padded)
+            inner_stage[n] = jnp.broadcast_to(inner[part], (padded, 128)).T[:8]
+            stage_ref[n] = darrived[part].astype(bf16)
+        for copy in sends(both[0], me):
+            copy.start()
+
+        @pl.when(turn + 1 < turns)
         def _():
-            for copy in sends(i, me):
+            for copy in sends(both[1], me):
                 copy.start()
 
         return carry
 
-    lax.fori_loop(0, sources, source, 0)
+    lax.fori_loop(0, turns, source, 0)
     back_ref[me] = stage_ref[me]
     inner_back[me] = inner_stage[me]
     wide = next(n for n in (512, 256, 128) if hidden % n == 0)
@@ -883,7 +934,7 @@
                 bring[k].wait()
 
     mine, width = dx_ref.shape
-    chunk = 256 if n_prompt % 256 == 0 and mine % 256 == 0 else 128
+    chunk = next(n for n in (512, 256, 128) if n_prompt % n == 0 and mine % n == 0)
 
     def front_rows(first):
         have(0, 1)
@@ -1090,12 +1141,11 @@
     routes = jnp.concatenate([prompt_route[0], cont_route[0, 0]]).T
     routes = jnp.pad(routes, ((0, 6), (0, 0)), constant_values=-1)
     fixed = (units, ((n_prompt, cap_prompt), (n_cont, cap_cont)), experts, padded)
-    qkv_full, out_full, misc, w_in, x_other, target, cot_slots = front(
-        w_qkv, w_out, jnp.concatenate(extra, axis=1), expert_in, prompt_in[0], routes, prompt_cot[0], cont_cot[0, 0], fixed, cycle, group
+    qkv_full, out_full, misc, w_in, w_down, x_other, target, cot_slots = front(
+        w_qkv, w_out, jnp.concatenate(extra, axis=1), expert_in, expert_out, prompt_in[0], routes, prompt_cot[0], cont_cot[0, 0], fixed, cycle, group
     )
     w_in = lax.all_gather(w_in.reshape(-1, w_in.shape[2]), "depth", axis=0, tiled=True)
-    expert_out, qkv_full = lax.optimization_barrier((expert_out, qkv_full))
-    w_down = lax.all_to_all(expert_out, "team", split_axis=0, concat_axis=0, tiled=True)
+    w_down = lax.all_gather(w_down.reshape(-1, w_down.shape[2]), "depth", axis=0, tiled=True)
     cots = lax.all_to_all(cot_slots, ("expert", "team"), split_axis=0, concat_axis=0, tiled=True)
     cot = jnp.concatenate([prompt_cot[0], cont_cot[0, 0]]).astype(f32)
     router_full = misc[:, :experts]
@@ -1115,8 +1165,7 @@
     normed = (x_all * inverse_x * gain_attn).astype(bf16)
     qkv = jnp.dot(normed, qkv_full, preferred_element_type=f32).astype(bf16)
     heads_out, lse = attend(own_list, table, qkv, n_prompt, n_cont, group, head_size)
-    w_down, cots, heads_out = lax.optimization_barrier((w_down, cots, heads_out))
-    w_down = lax.all_gather(w_down.reshape(-1, w_down.shape[2]), "depth", axis=0, tiled=True)
+    cots, heads_out = lax.optimization_barrier((cots, heads_out))
 
     middle = x + jnp.dot(heads_out, out_full, preferred_element_type=f32)
     inverse_m = rms_inverse(middle)

time: 521 us -> 509 us (0.977)
  starting transfers between devices: 28.9 us -> 13.3 us
    pallas_call x1, Pallas kernels: 27 us -> 46.5 us  [front(): pl.pallas_call(functools.partial(front_rest_kernel, cycle, group, fixed,...]
    reduce_scatter x2, starting transfers between devices: 11 us -> 0.08 us  [scatter_expert(): lax.psum_scatter(grad, 'depth', scatter_dimension=0, tiled=True)]
    pallas_call x1, Pallas kernels: 35.6 us -> 26 us  [front(): pl.pallas_call(functools.partial(front_kernel, cycle, cut, hops), out_sha...]
    all_to_all x1 -> x0, waiting for transfers between devices: 8.96 us -> none  [per_device(): lax.all_to_all(expert_out, 'team', split_axis=0, concat_axis=0, tiled=True)]
    all_gather x1, waiting for transfers between devices: 0.01 us -> 7.7 us  [per_device(): lax.all_gather(w_down.reshape(-1, w_down.shape[2]), 'depth', axis=0, tile...]
  transfers between devices with their start and end apart: 8 -> 7, of which waited for: 1 -> 1; matrix products, arithmetic and copies ran while one was open for 14% -> 15% of each run, Pallas kernels for 52% -> 57%
where the time goes in v1:
time: 509 us; the launch traced here: 503 us
  Pallas kernels  371 us (73%)
  matrix products  54.6 us (11%)
  local copies, waits for them, and re-layouts  23.7 us (5%)
  other arithmetic  16.8 us (3%)
  between operations  14.5 us (3%)
  starting transfers between devices  13.3 us (3%)
  waiting for transfers between devices  8.47 us (2%)
    pallas_call x1, Pallas kernels, expert_back(): pl.pallas_call(functools.partial(expert_back_kernel, units, group, expert...  81.6 us
    pallas_call x1, Pallas kernels, expert_up(): pl.pallas_call(functools.partial(expert_up_kernel, units, group, experts,...  74.8 us
    pallas_call x1, Pallas kernels, finish(): pl.pallas_call(functools.partial(finish_kernel, cycle, group, n_prompt, u...  60.2 us
    pallas_call x1, Pallas kernels, attend_grad(): pl.pallas_call(functools.partial(attend_grad_kernel, n_prompt, n_cont, gr...  48.7 us
    pallas_call x1, Pallas kernels, front(): pl.pallas_call(functools.partial(front_rest_kernel, cycle, group, fixed,...  46.5 us
    pallas_call x1, Pallas kernels, attend(): pl.pallas_call(functools.partial(attend_kernel, n_prompt, n_cont, group,...  33.6 us
    pallas_call x1, Pallas kernels, front(): pl.pallas_call(functools.partial(front_kernel, cycle, cut, hops), out_sha...  26 us
    dot_general x1, matrix products, per_device(): jnp.dot(active.reshape(-1, active.shape[2]), w_down, preferred_element_ty...  17.9 us
  transfers between devices with their start and end apart: 7, of which 1 were waited for; matrix products, arithmetic and copies ran while one was open for 15% of the time, Pallas kernels for 57%

profile of v1, /device:TPU:0, one launch (start us, length us, event | category | flops | bytes accessed | tf_op | source)
XLA Modules:
  0.0 502.9 jit_solution(9490650038726638891)
XLA Ops:
  7.2 0.7 reshape.130
  8.0 0.1 copy.53
  8.1 0.8 copy.52
  8.8 0.8 copy.50
  9.6 0.8 copy.51
  10.4 0.7 concatenate.25.extra_ref
  11.1 26.0 %front.1 = (bf16[8,2,48,2304]{3,2,1,0:T(8,128)(2,1)}, bf16[8,2,48,768]{3,2,1,0:T(8,128)(2,1)}, bf16[8,2,48,128]{3,2,1,0:T(8,128)(2,1)}, bf16[4,48,3072]{2,1,0:T(8,128)(2,1)}) custom-call(bf16[48,2304]{1,0:T(8,128)(2,1)} %qkv_ref.1, bf16[48,768]{1,0:T(8,128)(2,1)} %wout_ref.1, bf16[48,128]{1,0:T(8,128)(2,1)} %concatenate.25.extra_ref, ...), custom_call_target="tpu_custom_call" | custom-call | flops 10000000000 | bytes 100000000 | tf_op jit(solution)/shard_map/front/pallas_call | solution.py:474
  37.2 0.6 pad.19.routes_ref
  37.8 46.5 %front_rest.1 = (bf16[8,2,48,2304]{3,2,1,0:T(8,128)(2,1)}, bf16[8,2,48,768]{3,2,1,0:T(8,128)(2,1)}, bf16[8,2,48,128]{3,2,1,0:T(8,128)(2,1)}, bf16[4,192,768]{2,1...) custom-call(bf16[8,2,48,2304]{3,2,1,0:T(8,128)(2,1)} %get-tuple-elem, ...), custom_call_target="tpu_custom_call", output_to_operand_aliasing={{0}: (0, {}), {1}: (1, {}), {2}: (2, {})} | custom-call | flops 10000000000 | bytes 100000000 | tf_op jit(solution)/shard_map/front_rest/pallas_call | solution.py:484
  84.3 4.7 all-to-all-start
  89.1 0.7 all-gather.5.cloned.1.call-update
  89.8 0.3 fusion.22
  90.2 0.1 copy.69
  90.4 2.8 fusion.21
  93.1 0.5 multiply_reduce_fusion
  93.8 8.3 %convolution_convert_fusion.q_ref.k_ref.v_ref = bf16[1536,2304]{1,0:T(8,128)(2,1)} fusion(bf16[768,2304]{1,0:T(8,128)(2,1)S(1)} %bitcast.101, f32[768]{0:T(1024)S(1)} %convert_reduce_fusion.1, f32[1536]{0:T(1024)S(1)} %add_rsqrt_fusion, bf16[1536,768]{1,0:T(8,128)(2,1)S(1)} %get-tuple-element.127.refs_9_), kind=kOutput, calls=%fused_computation | convolution fusion | flops 5444075520 | bytes 12985344 | tf_op jit(solution)/shard_map/dot_general | solution.py:1166
  102.1 0.1 copy.71
  102.2 0.1 reshape_squeeze.6
  102.4 0.2 fusion.4
  102.6 0.7 reshape.133.table_ref
  103.3 33.6 %attend.1 = (bf16[1024,768]{1,0:T(8,128)(2,1)}, f32[6,2,1024]{2,1,0:T(2,128)}) custom-call(s32[1]{0:T(128)} %bitcast.own_ref, f32[6,2,2560]{2,1,0:T(2,128)} %reshape.133.table_ref, bf16[1536,2304]{1,0:T(8,128)(2,1)} %convolution_convert_fusion.q_ref.k_ref.v_ref, bf16[1536,2304]{1,0:T(8,128)(2,1)} %convolution_convert_fusion.q_ref.k_ref.v_ref, ...), custom_call_target="tpu_custom_call" | custom-call | flops 16106127360 | bytes 12582912 | tf_op jit(solution)/shard_map/attend/pallas_call | solution.py:182
  137.0 4.2 multiply_reduce_fusion.3
  141.2 0.3 multiply_convert_fusion.1.z_ref
  141.6 1.4 copy-done.1
  142.9 0.5 select_reduce_fusion
  143.5 0.6 pad.20.gate_ref.refs_6_
  144.1 74.8 %expert_up.1 = (bf16[8,320,3072]{2,1,0:T(8,128)(2,1)}, bf16[8,320,3072]{2,1,0:T(8,128)(2,1)}, bf16[3072,768]{1,0:T(8,128)(2,1)}, bf16[8,320,768]{2,1,0:T(8,128)(2,1)}, bf16[768,2560]{1,0:T(8,128)(2,1)}) custom-call(s32[8,1024]{1,0:T(8,128)} %get-tuple-element.59.target_ref.refs_5_, f32[8,1024]{1,0:T(8,128)} %pad.20.gate_ref.refs_6_, ...), custom_call_target="tpu_custom_call" | custom-call | flops 36238786560 | bytes 100000000 | tf_op jit(solution)/shard_map/expert_up/pallas_call | solution.py:629
  219.1 0.6 pad.25.clone
  219.7 7.7 %all-gather.5.cloned.1.call-done.w_down_ref = bf16[3072,768]{1,0:T(8,128)(2,1)} async-done(((bf16[768,768]{1,0:T(8,128)(2,1)}), bf16[3072,768]{1,0:T(8,128)(2,1)}) %all-gather.5.cloned.1.call-update) | async-done | bytes 4718608 | tf_op jit(solution)/shard_map/all_gather | solution.py:1148
  227.4 81.6 %expert_back.1 = (bf16[768,3072]{1,0:T(8,128)(2,1)}, f32[1024,768]{1,0:T(8,128)}, f32[8,1024]{1,0:T(8,128)}) custom-call(s32[8,1024]{1,0:T(8,128)} %get-tuple-element.59.target_ref.refs_5_, bf16[8,320,768]{2,1,0:T(8,128)(2,1)} %get-tuple-element.62.dproduced_hbm, bf16[8,320,3072]{2,1,0:T(8,128)(2,1)} %get-tuple-element.63.slope_hbm, ...), custom_call_target="tpu_custom_call" | custom-call | flops 36238786560 | bytes 100000000 | tf_op jit(solution)/shard_map/expert_back/pallas_call | solution.py:805
  309.0 0.8 slice_reduce_fusion.3
  309.8 0.8 multiply_subtract_fusion
  310.6 4.5 multiply_reduce_fusion.1
  315.2 3.2 multiply_add_fusion.refs_10_
  318.4 1.7 copy-done.7
  320.1 2.6 convolution_convert_fusion.3.do_ref
  322.7 3.9 all-to-all-start.1
  326.7 17.9 %convolution_convert_fusion.1 = bf16[2560,768]{1,0:T(8,128)(2,1)} fusion(bf16[2560,3072]{1,0:T(8,128)(2,1)} %bitcast.98, bf16[3072,768]{1,0:T(8,128)(2,1)} %all-gather.5.cloned.1.call-done.w_down_ref), kind=kOutput, calls=%fused_computation.1 | convolution fusion | flops 12081561600 | bytes 24379392 | tf_op jit(solution)/shard_map/dot_general | solution.py:1204
  344.5 0.3 fusion.1
  344.9 0.8 copy.61
  345.7 0.8 broadcast_in_dim.62
  346.6 4.4 convolution_convert_fusion.4
  350.9 4.5 all-to-all-start.2
  355.5 48.7 %attend_grad.1 = (bf16[3,1536,768]{2,1,0:T(8,128)(2,1)}, f32[6,2,2560]{2,1,0:T(2,128)}) custom-call(s32[1]{0:T(128)} %bitcast.own_ref, f32[6,2,2560]{2,1,0:T(2,128)} %reshape.133.table_ref, bf16[1536,2304]{1,0:T(8,128)(2,1)} %convolution_convert_fusion.q_ref.k_ref.v_ref, bf16[1536,2304]{1,0:T(8,128)(2,1)} %convolution_convert_fusion.q_ref.k_ref.v_ref, ...), custom_call_target="tpu_custom_call" | custom-call | flops 40265318400 | bytes 31457280 | tf_op jit(solution)/shard_map/attend_grad/pallas_call | solution.py:208
  404.2 1.7 reshape.142
  405.9 1.0 convolution_convert_fusion.5
  406.9 0.1 copy.60
  407.2 0.9 reshape.151
  408.1 2.0 maximum_maximum_fusion
  410.1 10.6 %convolution_convert_fusion.2 = bf16[3,768,768]{1,2,0:T(8,128)(2,1)} fusion(bf16[3,1536,768]{2,1,0:T(8,128)(2,1)} %get-tuple-element.73.refs_7_, f32[768]{0:T(1024)S(1)} %copy-done.19, f32[1536]{0:T(1024)} %copy-done.20, bf16[1536,768]{1,0:T(8,128)(2,1)S(1)} %copy-done.4), kind=kOutput, calls=%fused_computation.10 | convolution fusion | flops 5442306048 | bytes 12985344 | tf_op jit(solution)/shard_map/rd,cre->cde/dot_general | solution.py:1211
  420.7 0.6 broadcast_in_dim.57.refs_4_
  421.4 60.2 %finish.1 = (f32[48,2304]{1,0:T(8,128)}, f32[48,768]{1,0:T(8,128)}, f32[48,128]{1,0:T(8,128)}, bf16[4,48,3072]{2,1,0:T(8,128)(2,1)}, f32[1024,768]{1,0:T(8,128)}, /*index=5*/bf16[1024,768]{1,0:T(8,128)(2,1)}) custom-call(bf16[3,8,2,48,768]{4,3,2,1,0:T(8,128)(2,1)} %bitcast.99, bf16[1,8,2,48,768]{4,3,2,1,0:T(8,128)(2,1)} %bitcast.102, ...), custom_call_target="tpu_custom_call" | custom-call | flops 30000001024 | bytes 100000000 | tf_op jit(solution)/shard_map/finish/pallas_call | solution.py:1018
  481.6 1.3 multiply_reduce_fusion.4
  482.8 0.9 slice_reduce_fusion.2
  483.7 1.4 slice_reduce_fusion.1
  485.2 1.6 convert_element_type.114
  486.8 1.2 slice_bitcast_fusion.2
  488.0 0.5 convert_divide_fusion
  488.5 0.6 reshape_squeeze.7
  489.2 0.7 copy.64
  489.9 2.9 convert_element_type.113
  492.8 1.9 slice_bitcast_fusion
  494.7 0.8 copy.78
  495.4 0.7 copy.79
  (85 shorter events, 0.9 us)
Async XLA Ops:
  7.2 137.0 %all-gather.3.cloned.1.call-start = ((), (), s32[]{:S(2)}) async-start(), calls=%async_computation.5 | async-start | bytes 5898240 | tf_op jit(solution)/shard_map/all_gather | solution.py:1147
  11.1 26.1 %copy-start.21 = (s32[1,1,512,2]{2,3,1,0:T(2,128)S(1)}, s32[1,1,512,2]{2,3,1,0:T(2,128)}, u32[]{:S(2)}) copy-start(s32[1,1,512,2]{2,3,1,0:T(2,128)} %param.20) | copy-start | bytes 12292
  11.1 26.1 %copy-start.22 = (s32[1,512,2]{1,2,0:T(2,128)S(1)}, s32[1,512,2]{1,2,0:T(2,128)}, u32[]{:S(2)}) copy-start(s32[1,512,2]{1,2,0:T(2,128)} %param.19) | copy-start | bytes 12292
  84.3 5.5 %copy-start.5 = (bf16[8,2,48,128]{3,2,1,0:T(8,128)(2,1)S(1)}, bf16[8,2,48,128]{3,2,1,0:T(8,128)(2,1)}, u32[]{:S(2)}) copy-start(bf16[8,2,48,128]{3,2,1,0:T(8,128)(2,1)} %get-tuple-element.52) | copy-start | bytes 589828
  84.3 6.0 %copy-start.10 = (bf16[1,512,768]{2,1,0:T(8,128)(2,1)S(1)}, bf16[1,512,768]{2,1,0:T(8,128)(2,1)}, u32[]{:S(2)}) copy-start(bf16[1,512,768]{2,1,0:T(8,128)(2,1)} %param.15) | copy-start | bytes 2359300
  84.3 6.0 %copy-start.11 = (bf16[1,1,512,768]{3,2,1,0:T(8,128)(2,1)S(1)}, bf16[1,1,512,768]{3,2,1,0:T(8,128)(2,1)}, u32[]{:S(2)}) copy-start(bf16[1,1,512,768]{3,2,1,0:T(8,128)(2,1)} %param.16) | copy-start | bytes 2359300
  84.3 6.0 %copy-start.12 = (bf16[1,512,768]{2,1,0:T(8,128)(2,1)S(1)}, bf16[1,512,768]{2,1,0:T(8,128)(2,1)}, u32[]{:S(2)}) copy-start(bf16[1,512,768]{2,1,0:T(8,128)(2,1)} %get-tuple-element.53) | copy-start | bytes 2359300
  84.3 52.6 %all-to-all-start = ((bf16[8,320,768]{2,1,0:T(8,128)(2,1)}), bf16[8,320,768]{2,1,0:T(8,128)(2,1)}, u32[]{:S(2)}, u32[]{:S(2)}) async-start(bf16[8,320,768]{2,1,0:T(8,128)(2,1)} %get-tuple-element.55), calls=%async_computation | async-start | bytes 7864320 | tf_op jit(solution)/shard_map/all_to_all | solution.py:1149
  89.0 138.4 %all-gather.5.cloned.1.call-start = ((), (), s32[]{:S(2)}) async-start(), calls=%async_computation.6 | async-start | bytes 5898240 | tf_op jit(solution)/shard_map/all_gather | solution.py:1148
  89.8 232.9 %reduce-scatter.3.cloned.1.call-start = ((), (), s32[]{:S(2)}) async-start(), calls=%async_computation.7 | async-start | bytes 5898240 | tf_op jit(solution)/shard_map/reduce_scatter | solution.py:1066
  90.3 3.4 copy-start.18
  90.4 3.4 copy-start.24
  93.1 8.9 %copy-start.3 = (bf16[1536,768]{1,0:T(8,128)(2,1)}, bf16[1536,768]{1,0:T(8,128)(2,1)S(1)}, u32[]{:S(2)}) copy-start(bf16[1536,768]{1,0:T(8,128)(2,1)S(1)} %get-tuple-element.127.refs_9_) | copy-start | bytes 7077892
  93.7 8.4 %copy-start.20 = (f32[1536]{0:T(1024)}, f32[1536]{0:T(1024)S(1)}, u32[]{:S(2)}) copy-start(f32[1536]{0:T(1024)S(1)} %add_rsqrt_fusion) | copy-start | bytes 18436
  93.8 8.6 %copy-start.16 = (s32[1536]{0:T(1024)S(1)}, s32[1536]{0:T(1024)}, u32[]{:S(2)}) copy-start(s32[1536]{0:T(1024)} %param.21) | copy-start | bytes 18436
  141.2 174.0 %copy-start = (f32[1024,768]{1,0:T(8,128)}, f32[1024,768]{1,0:T(8,128)S(1)}, u32[]{:S(2)}) copy-start(f32[1024,768]{1,0:T(8,128)S(1)} %get-tuple-element.143.refs_11_) | copy-start | bytes 9437188
  141.5 1.4 copy-start.1
  219.0 201.7 %reduce-scatter.5.cloned.1.call-start = ((), (), s32[]{:S(2)}) async-start(), calls=%async_computation.8 | async-start | bytes 5898240 | tf_op jit(solution)/shard_map/reduce_scatter | solution.py:1066
  315.2 4.9 copy-start.25
  318.4 1.7 copy-start.7
  322.7 28.2 %all-to-all-start.1 = ((bf16[4,192,768]{2,1,0:T(8,128)(2,1)}), bf16[4,192,768]{2,1,0:T(8,128)(2,1)S(1)}, u32[]{:S(2)}, u32[]{:S(2)}) async-start(bf16[4,192,768]{2,1,0:T(8,128)(2,1)} %bitcast.69), calls=%async_computation.2 | async-start | bytes 2359296 | tf_op jit(solution)/shard_map/all_to_all | solution.py:1208
  326.6 17.9 %copy-start.2 = (bf16[1024,768]{1,0:T(8,128)(2,1)S(1)}, bf16[1024,768]{1,0:T(8,128)(2,1)}, u32[]{:S(2)}) copy-start(bf16[1024,768]{1,0:T(8,128)(2,1)} %copy-done.1) | copy-start | bytes 4718596
  326.6 19.9 %copy-start.26 = (bf16[1024,768]{1,0:T(8,128)(2,1)S(1)}, bf16[1024,768]{1,0:T(8,128)(2,1)}, u32[]{:S(2)}) copy-start(bf16[1024,768]{1,0:T(8,128)(2,1)} %get-tuple-element.57.o_ref) | copy-start | bytes 4718596
  350.9 69.8 %all-to-all-start.2 = ((bf16[8,320,768]{2,1,0:T(8,128)(2,1)}), bf16[8,320,768]{2,1,0:T(8,128)(2,1)}, u32[]{:S(2)}, u32[]{:S(2)}) async-start(bf16[8,320,768]{2,1,0:T(8,128)(2,1)} %bitcast.66), calls=%async_computation.4 | async-start | bytes 7864320 | tf_op jit(solution)/shard_map/all_to_all | solution.py:1206
  355.5 50.4 %copy-start.17 = (s32[1536]{0:T(1024)S(1)}, s32[1536]{0:T(1024)}, u32[]{:S(2)}) copy-start(s32[1536]{0:T(1024)} %param.21) | copy-start | bytes 18436
  355.5 54.6 %copy-start.4 = (bf16[1536,768]{1,0:T(8,128)(2,1)S(1)}, bf16[1536,768]{1,0:T(8,128)(2,1)}, u32[]{:S(2)}) copy-start(bf16[1536,768]{1,0:T(8,128)(2,1)} %copy-done.3) | copy-start | bytes 7077892
  355.5 54.6 %copy-start.19 = (f32[768]{0:T(1024)S(1)}, f32[768]{0:T(1024)}, u32[]{:S(2)}) copy-start(f32[768]{0:T(1024)} %copy-done.18) | copy-start | bytes 9220
  421.3 60.2 %copy-start.13 = (bf16[48,2304]{1,0:T(8,128)(2,1)S(1)}, bf16[48,2304]{1,0:T(8,128)(2,1)}, u32[]{:S(2)}) copy-start(bf16[48,2304]{1,0:T(8,128)(2,1)} %qkv_ref.1) | copy-start | bytes 663556
  481.5 5.2 %copy-start.9 = (bf16[1024,768]{1,0:T(8,128)(2,1)S(1)}, bf16[1024,768]{1,0:T(8,128)(2,1)}, u32[]{:S(2)}) copy-start(bf16[1024,768]{1,0:T(8,128)(2,1)} %get-tuple-element.79) | copy-start | bytes 4718596
  485.2 2.9 copy-start.23
  485.2 4.0 copy-start.14
  486.8 6.0 %copy-start.6 = (f32[1024,768]{1,0:T(8,128)S(1)}, f32[1024,768]{1,0:T(8,128)}, u32[]{:S(2)}) copy-start(f32[1024,768]{1,0:T(8,128)} %get-tuple-element.80) | copy-start | bytes 9437188
  492.8 1.9 copy-start.8
  492.8 2.6 copy-start.15
Sparse Core Ops, SparseCore 0:
  37.3 100.5 all-gather.2
  139.4 87.9 all-gather.4
  229.8 85.0 reduce-scatter.2
  317.0 85.7 reduce-scatter.4
